TPU v7x, 32 devices: a whole 2x2x4 slice. The times are simulated.
32 devices in a mesh: clip: 8 (over z, core), row: 4 (over y, x).
Axes of the slice: x: 2, y: 2, z: 4, core: 2. Of those that a mesh axis runs over, the one named last changes fastest.
Arguments:
- inputs: bfloat16 [32768, 384], P(('clip', 'row')), may hold values from -6 to 6
- cotangent: bfloat16 [32768, 384], P(('clip', 'row')), may hold values from -6 to 6
- source_of: int32 [32768], P(('clip', 'row')), may hold values from 0 to 32767, as said below
- split_row: int32 [8], P('clip'), may hold values from 32 to 64, as said below
- qkv_weight: bfloat16 [2, 384, 1152], P(None, 'row'), may hold values from -0.3125 to 0.3125
- qv_bias: bfloat16 [2, 2, 384], P(None, None, 'row'), may hold values from -3 to 3
- proj_weight: bfloat16 [2, 384, 384], P(None, 'row'), may hold values from -1.25 to 1.25
- proj_bias: bfloat16 [2, 384], P(None, 'row'), may hold values from -2 to 2
- fc1_weight: bfloat16 [2, 384, 1536], P(None, 'row'), may hold values from -0.3125 to 0.3125
- fc1_bias: bfloat16 [2, 1536], P(None, 'row'), may hold values from -2 to 2
- fc2_weight: bfloat16 [2, 1536, 384], P(None, 'row'), may hold values from -0.21875 to 0.21875
- fc2_bias: bfloat16 [2, 384], P(None, 'row'), may hold values from -2 to 2
- norm_gain: bfloat16 [2, 2, 384], P(None, None, 'row'), may hold values from 0.25 to 1.75
- norm_bias: bfloat16 [2, 2, 384], P(None, None, 'row'), may hold values from -2 to 2
- rel_table: float32 [2, 225, 16], replicated, may hold values from -3 to 3
Outputs:
- output: bfloat16 [32768, 384], P(('clip', 'row'))
- input_grad: float32 [32768, 384], P(('clip', 'row'))
- qkv_grad: float32 [2, 384, 1152], P(None, 'row')
- qv_bias_grad: float32 [2, 2, 384], P(None, None, 'row')
- proj_grad: float32 [2, 384, 384], P(None, 'row')
- proj_bias_grad: float32 [2, 384], P(None, 'row')
- fc1_grad: float32 [2, 384, 1536], P(None, 'row')
- fc1_bias_grad: float32 [2, 1536], P(None, 'row')
- fc2_grad: float32 [2, 1536, 384], P(None, 'row')
- fc2_bias_grad: float32 [2, 384], P(None, 'row')
- gain_grad: float32 [2, 2, 384], P(None, None, 'row')
- norm_bias_grad: float32 [2, 2, 384], P(None, None, 'row')
- table_grad: float32 [2, 225, 16], replicated
Inputs may be any that keep to these rules, and one draw needn't show every extreme that they name: `source_of`: A permutation; the slot-layout rows of the device with index j of clip+row have sources on every device, 32 from each, and on device s these sources are its rows j * 32 to (j + 1) * 32 - 1. `split_row`: each entry is 32 or 64; both values occur in every draw.
All inputs are finite; a program needn't handle non-finite values.
Results may differ from a plain program's by a relative error of at most 0.023.
Values may be sent and summed in bfloat16 or wider, within the bound.
A program may use at most 192 MiB of HBM per device.

v0:
```python
import functools

import jax
import jax.numpy as jnp
import numpy as np
from jax import lax
from jax.experimental import pallas as pl
from jax.experimental.pallas import tpu as pltpu
from jax.sharding import PartitionSpec as P

WIN = 8
SHIFT = 4
GRID_COLS = 64
EPSILON = 1e-05
MASKED = -1000000000.0
ROOT_HALF = 0.7071067811865476
INV_ROOT_TAU = 0.3989422804014327

HEADS = 16
HEAD_DIM = 24
D = HEADS * HEAD_DIM
GROUP = 8
CELL = WIN * WIN
BLOCK = SHIFT * SHIFT
WIN_COLS = GRID_COLS // WIN
SPREAD = 2 * WIN - 1
TABLE = SPREAD * SPREAD
TABLE_PAD = 256
SCALE = HEAD_DIM**-0.5
CHUNK = 256
CHUNK_WINS = CHUNK // CELL
VMEM_LIMIT = 56 * 1024 * 1024

MESH = pl.DeviceIdType.MESH
f32 = jnp.float32
bf16 = jnp.bfloat16


def window_places():
    spot = np.arange(CELL)
    row = (spot // 32) * SHIFT + (spot % BLOCK) // SHIFT
    col = (spot // BLOCK % 2) * SHIFT + spot % SHIFT
    return row, col


def head_masks():
    feature = np.arange(D) // HEAD_DIM
    rows = (feature[None, :] == np.arange(HEADS)[:, None]).astype(np.float32)
    wide = np.stack(
        [
            np.repeat(rows[GROUP * g : GROUP * (g + 1), 128 * g : 128 * g + 256], CELL, axis=0)
            for g in range(2)
        ]
    )
    return rows, wide


def table_constants():
    row, col = window_places()
    natural = row * WIN + col
    lanes = np.zeros((2, TABLE_PAD, 128), np.float32)
    for half in range(2):
        lanes[half, row * SPREAD + col, half * CELL + np.arange(CELL)] = 1.0
    order = np.zeros((CELL, CELL), np.float32)
    order[np.arange(CELL), natural] = 1.0
    back = np.zeros((CELL, CELL), np.float32)
    back[row * WIN + (WIN - 1 - col), np.arange(CELL)] = 1.0
    return lanes, order, back


def dot_nn(a, b):
    return lax.dot_general(a, b, (((1,), (0,)), ((), ())), preferred_element_type=f32)


def dot_nt(a, b):
    return lax.dot_general(a, b, (((1,), (1,)), ((), ())), preferred_element_type=f32)


def dot_tn(a, b):
    return lax.dot_general(a, b, (((0,), (0,)), ((), ())), preferred_element_type=f32)


def dot_exact(a, b, dims):
    return lax.dot_general(
        a, b, (dims, ((), ())), precision=lax.Precision.HIGHEST, preferred_element_type=f32
    )


def split(values):
    high = values.astype(bf16)
    rest = values - high.astype(f32)
    middle = rest.astype(bf16)
    return high, middle, (rest - middle.astype(f32)).astype(bf16)


def whole(shape):
    zeros = (0,) * len(shape)
    return pl.BlockSpec(shape, lambda i: zeros)


def rows_of(shape):
    return pl.BlockSpec(shape, lambda i: (i, 0))


def norm_parts(values):
    centred = values - jnp.mean(values, axis=-1, keepdims=True)
    inverse = lax.rsqrt(jnp.mean(centred * centred, axis=-1, keepdims=True) + EPSILON)
    return centred * inverse, inverse


def norm_back(upstream, normal, inverse, gain):
    scaled = upstream * gain
    centred = scaled - jnp.mean(scaled, axis=-1, keepdims=True)
    return inverse * (centred - normal * jnp.mean(scaled * normal, axis=-1, keepdims=True))


def column_sum(values):
    return jnp.sum(values, axis=0, keepdims=True)


def bias_rows(table_ref, lanes_ref, order_ref, out_ref, wide_ref):
    for layer in range(2):
        for head in range(HEADS):
            pair, half = divmod(head, 2)
            spread = jnp.broadcast_to(table_ref[layer, head : head + 1, :], (WIN, TABLE_PAD))
            for i in range(WIN):
                at = CELL * pair + WIN * i
                wide_ref[at : at + WIN, TABLE_PAD * half : TABLE_PAD * (half + 1)] = pltpu.roll(
                    spread, (SPREAD * i - 112) % TABLE_PAD, 1, stride=1, stride_axis=0
                )
        picked = sum(dot_nn(part, lanes_ref[...]) for part in reversed(split(wide_ref[...])))
        joined = jnp.concatenate(
            [picked[CELL * pair : CELL * (pair + 1), :] for pair in range(HEADS // 2)], axis=1
        )
        out_ref[layer] = sum(dot_nn(order_ref[...], part) for part in reversed(split(joined)))


def table_rows(grads, lanes_ref, back_ref):
    turned = sum(dot_nn(back_ref[...], part) for part in reversed(split(grads)))
    stacked = jnp.concatenate([turned[:, 128 * i : 128 * (i + 1)] for i in range(HEADS // 2)], axis=0)
    spread = sum(dot_nt(part, lanes_ref[...]) for part in reversed(split(stacked)))
    rows = []
    for head in range(HEADS):
        pair, half = divmod(head, 2)
        total = jnp.zeros((WIN, TABLE_PAD), f32)
        for i in range(WIN):
            at = CELL * pair + WIN * i
            total += pltpu.roll(
                spread[at : at + WIN, TABLE_PAD * half : TABLE_PAD * (half + 1)],
                (112 - SPREAD * i - (WIN - 1)) % TABLE_PAD,
                1,
                stride=1,
                stride_axis=0,
            )
        rows.append(column_sum(total))
    return jnp.concatenate(rows, axis=0)


def quarter(window, sub):
    return pl.ds(CELL * window + BLOCK * sub, BLOCK)


def assemble_back(main_ref, edge_ref, out_ref):
    windows = main_ref.shape[0] // CELL
    for window in range(windows):
        wr, wc = divmod(window, WIN_COLS)
        before = (wc - 1) % WIN_COLS
        out_ref[quarter(window, 3), :] = main_ref[quarter(window, 0), :].astype(out_ref.dtype)
        out_ref[quarter(window, 2), :] = main_ref[
            quarter(wr * WIN_COLS + before, 1), :
        ].astype(out_ref.dtype)
        for sub, col, piece in ((1, wc, 0), (0, before, 1)):
            if wr == 0:
                value = edge_ref[pl.ds(2 * BLOCK * col + BLOCK * piece, BLOCK), :]
            else:
                value = main_ref[quarter((wr - 1) * WIN_COLS + col, 2 + piece), :]
            out_ref[quarter(window, sub), :] = value.astype(out_ref.dtype)


def assemble_ahead(main_ref, edge_ref, out_ref):
    windows = main_ref.shape[0] // CELL
    last = windows // WIN_COLS - 1
    for window in range(windows):
        wr, wc = divmod(window, WIN_COLS)
        after = (wc + 1) % WIN_COLS
        out_ref[quarter(window, 0), :] = main_ref[quarter(window, 3), :].astype(out_ref.dtype)
        out_ref[quarter(window, 1), :] = main_ref[
            quarter(wr * WIN_COLS + after, 2), :
        ].astype(out_ref.dtype)
        for sub, col, piece in ((2, wc, 1), (3, after, 0)):
            if wr == last:
                value = edge_ref[pl.ds(2 * BLOCK * col + BLOCK * piece, BLOCK), :]
            else:
                value = main_ref[quarter((wr + 1) * WIN_COLS + col, piece), :]
            out_ref[quarter(window, sub), :] = value.astype(out_ref.dtype)


class Place:
    def __init__(self, n_row, n_far):
        clip = lax.axis_index("clip")
        self.n_row, self.n_far = n_row, n_far
        self.core, self.far, self.row = clip % 2, clip // 2, lax.axis_index("row")
        self.n = 2 * n_far * n_row
        self.index = clip * n_row + self.row

    def index_at(self, d):
        return (self.index + d) % self.n

    def device(self, d):
        at = self.index_at(d)
        return (at // self.n_row, at % self.n_row)

    def row_at(self, d):
        return (self.row + d) % self.n_row

    def far_at(self, d):
        return (self.far + d) % self.n_far

    def twin(self):
        return (2 * self.far + 1 - self.core, self.row)

    def in_row(self, d):
        return (2 * self.far + self.core, self.row_at(d))

    def along(self, d):
        return (2 * self.far_at(d) + self.core, self.row)

    def partners(self, far=True):
        found = [self.twin()] + [self.in_row(d) for d in range(1, self.n_row)]
        return found + ([self.along(d) for d in range(1, self.n_far)] if far else [])


def meet(partners):
    barrier = pltpu.get_barrier_semaphore()
    for partner in partners:
        pl.semaphore_signal(barrier, inc=1, device_id=partner, device_id_type=MESH)
    pl.semaphore_wait(barrier, len(partners))


def send(src, dst, send_sem, recv_sem, target):
    copy = pltpu.make_async_remote_copy(
        src_ref=src,
        dst_ref=dst,
        send_sem=send_sem,
        recv_sem=recv_sem,
        device_id=target,
        device_id_type=MESH,
    )
    copy.start()
    return copy


def remote(src, dst, send_sem, recv_sem, target):
    return pltpu.make_async_remote_copy(
        src_ref=src,
        dst_ref=dst,
        send_sem=send_sem,
        recv_sem=recv_sem,
        device_id=target,
        device_id_type=MESH,
    )


def can_swap(tokens, n):
    return tokens // n % 16 == 0


def meet_all(place):
    barrier = pltpu.get_barrier_semaphore()

    def greet(d, carry):
        pl.semaphore_signal(barrier, inc=1, device_id=place.device(d), device_id_type=MESH)
        return carry

    lax.fori_loop(1, place.n, greet, 0)
    pl.semaphore_wait(barrier, place.n - 1)


def swap_block(place, ref, index):
    count = ref.shape[0] // place.n
    return ref.at[pl.ds(pl.multiple_of(index * count, 16), count), :]


def swap_own(place, src, dst, sem):
    return pltpu.make_async_copy(
        swap_block(place, src, place.index), swap_block(place, dst, place.index), sem.at[0, 0]
    )


def swap_copy(place, src, dst, sem, d, owner):
    return remote(
        swap_block(place, src, place.index_at(d)),
        swap_block(place, dst, owner),
        sem.at[0, d],
        sem.at[1, d],
        place.device(d),
    )


def swap_start(place, src, dst, sem):
    def work(d, carry):
        swap_copy(place, src, dst, sem, d, place.index).start()
        return carry

    lax.fori_loop(1, place.n, work, 0)


def swap_wait(place, src, dst, sem):
    def work(d, carry):
        swap_copy(place, src, dst, sem, d, place.index_at(place.n - d)).wait_recv()
        return carry

    lax.fori_loop(1, place.n, work, 0)


def swap_end(place, src, dst, sem):
    def work(d, carry):
        swap_copy(place, src, dst, sem, d, place.index).wait_send()
        return carry

    lax.fori_loop(1, place.n, work, 0)


def row_share(n_row):
    return D // n_row


HALVES = (((0, 0, 1), (1, 0, 1), (3, 0, 2)), ((2, 0, 1), (3, 2, 2)))
HEIGHTS = (1, 1, 1, 4)


def forward_kernel(
    n_row,
    n_far,
    swap,
    cuts_ref,
    place_col,
    place_row,
    x_in,
    c_in,
    qkv_i,
    proj_i,
    fc1_i,
    fc2_i,
    vec_i,
    table_ref,
    lanes_ref,
    order_ref,
    heads_ref,
    wide_heads_ref,
    x_out,
    qkv_out,
    prob_out,
    att_out,
    mid_out,
    act_out,
    slope_out,
    up_out,
    rows_out,
    qkv_wo,
    proj_wo,
    fc1_wo,
    fc2_wo,
    vec_out,
    x_got,
    c_got,
    qkv_s,
    proj_s,
    fc1_s,
    fc2_s,
    vec_got,
    qkv_b,
    fc1_b,
    bias_s,
    wide_s,
    x_s,
    y_s,
    c_s,
    edge_out,
    edge_in,
    x_sem,
    c_sem,
    own_sem,
    row_sem,
    twin_sem,
    vec_sem,
    edge_sem,
    out_sem,
):
    step = pl.program_id(0)
    tokens = x_s.shape[0]
    chunks = tokens // CHUNK
    layer = step // chunks
    chunk = (step + layer * (chunks // 2)) % chunks
    place = Place(n_row, n_far)
    size = row_share(n_row)
    shards = (qkv_i, proj_i, fc1_i, fc2_i)
    kept = (qkv_s, proj_s, fc1_s, fc2_s)
    outs = (qkv_wo, proj_wo, fc1_wo, fc2_wo)
    last_row = (tokens // CELL // WIN_COLS - 1) * WIN_COLS
    if not swap:
        x_got, c_got = x_in, c_in

    def own(l, w):
        return pltpu.make_async_copy(
            shards[w].at[l], spot(l, w, place.row, 0, HEIGHTS[w]), own_sem.at[l, w]
        )

    def spot(l, w, owner, first, count):
        at = pl.multiple_of((owner * HEIGHTS[w] + first) * size, 16)
        return kept[w].at[l, pl.ds(at, count * size), :]

    def push(l, core, i, d, source=None):
        w, first, count = HALVES[core][i]
        return remote(
            shards[w].at[l, pl.ds(first * size, count * size), :],
            spot(l, w, place.row if source is None else source, first, count),
            row_sem.at[0, l, i, d - 1],
            row_sem.at[1, l, i, d - 1],
            place.in_row(d),
        )

    def hand(l, core, i, d):
        w, first, count = HALVES[core][i]
        here = spot(l, w, place.row_at(n_row - d), first, count)
        return remote(
            here, here, twin_sem.at[0, l, i, d - 1], twin_sem.at[1, l, i, d - 1], place.twin()
        )

    def pieces(core):
        return [(i, d) for i in range(len(HALVES[core])) for d in range(1, n_row)]

    def by_core(work):
        for core in range(2):
            pl.when(place.core == core)(functools.partial(work, core))

    def start_weights(l):
        def work(core):
            for i, d in pieces(core):
                push(l, core, i, d).start()

        by_core(work)

    def pass_weights(l):
        def work(core):
            for i, d in pieces(core):
                push(l, core, i, d, place.row_at(n_row - d)).wait_recv()
                hand(l, core, i, d).start()

        by_core(work)

    def wait_weights(l):
        def work(core):
            for i, d in pieces(1 - core):
                hand(l, 1 - core, i, d).wait_recv()

        by_core(work)
        for w in range(4):
            own(l, w).wait()

    def end_weights(l):
        def work(core):
            for i, d in pieces(core):
                push(l, core, i, d).wait_send()
                hand(l, core, i, d).wait_send()

        by_core(work)

    def vector_copy(d):
        return remote(
            vec_i, vec_got.at[place.row], vec_sem.at[0, d - 1], vec_sem.at[1, d - 1], place.in_row(d)
        )

    def edge_copy(which, d):
        return remote(
            edge_out.at[which],
            edge_in.at[which],
            edge_sem.at[0, which],
            edge_sem.at[1, which],
            place.in_row(d),
        )

    def pack_edge(which, source, first_window, first_sub):
        for col in range(WIN_COLS):
            at = CELL * (first_window + col) + BLOCK * first_sub
            edge_out[which, 2 * BLOCK * col : 2 * BLOCK * (col + 1), :] = source[
                at : at + 2 * BLOCK, :
            ].astype(bf16)

    def pick_rows(source, target):
        for c in range(chunks):
            rows = slice(CHUNK * c, CHUNK * (c + 1))
            spots = lax.broadcasted_iota(jnp.int32, (CHUNK, tokens), 1)
            pick = jnp.where(spots == place_col[rows, :], 1.0, 0.0).astype(bf16)
            target[rows, :] = dot_nn(pick, source[...]).astype(target.dtype)

    @pl.when(step == 0)
    def _():
        for l in range(2):
            for w in range(4):
                own(l, w).start()
        mine = pltpu.make_async_copy(vec_i, vec_got.at[place.row], out_sem.at[4])
        mine.start()
        if swap:
            swap_own(place, x_in, x_got, x_sem).start()
            swap_own(place, c_in, c_got, c_sem).start()
            meet_all(place)
            swap_start(place, x_in, x_got, x_sem)
        else:
            meet(place.partners(far=False))
        for d in range(1, n_row):
            vector_copy(d).start()
        start_weights(0)
        bias_rows(table_ref, lanes_ref, order_ref, bias_s, wide_s)
        mine.wait()
        for d in range(1, n_row):
            vector_copy(d).wait()
        for l in range(2):
            shares = [vec_got[r, 16 * l : 16 * (l + 1), :].astype(f32) for r in range(n_row)]
            rows = jnp.concatenate([share[0:8, 0:size] for share in shares], axis=1)
            vec_out[l] = rows
            qkv_b[l, 0:1, 0:D] = rows[0:1]
            qkv_b[l, 0:1, D : 2 * D] = jnp.zeros((1, D), f32)
            qkv_b[l, 0:1, 2 * D : 3 * D] = rows[1:2]
            fc1_b[l, 0:1, :] = jnp.concatenate(
                [share[8:9, 0 : 4 * size] for share in shares], axis=1
            )
        if swap:
            swap_wait(place, x_in, x_got, x_sem)
            swap_own(place, x_in, x_got, x_sem).wait()
        pick_rows(x_got, x_s)
        pass_weights(0)
        wait_weights(0)

    @pl.when(step == 1)
    def _():
        start_weights(1)
        if swap:
            swap_start(place, c_in, c_got, c_sem)

    @pl.when(step == chunks - 1)
    def _():
        pass_weights(1)

    @pl.when(step == chunks)
    def _():
        wait_weights(1)
        for w in range(4):
            pltpu.make_async_copy(kept[w], outs[w], out_sem.at[w]).start()
        edge_copy(0, n_row - 1).wait_recv()
        assemble_ahead(y_s, edge_in.at[0], x_s)

    @pl.when(step == chunks + 2)
    def _():
        if swap:
            swap_wait(place, c_in, c_got, c_sem)
            swap_own(place, c_in, c_got, c_sem).wait()
        pick_rows(c_got, c_s)
        pack_edge(2, c_s, 0, 0)
        edge_copy(2, n_row - 1).start()

    here = pl.ds(pl.multiple_of(chunk * CHUNK, CHUNK), CHUNK)
    x = x_s[here, :]
    x_out[0] = x
    normal, _ = norm_parts(x)
    hidden = (normal * vec_out[layer, 4:5, :] + vec_out[layer, 6:7, :]).astype(bf16)
    qkv_out[0] = (dot_nn(hidden, qkv_s[layer]) + qkv_b[layer]).astype(bf16)
    wide = (CELL, GROUP * CELL)
    apart = lax.broadcasted_iota(jnp.int32, wide, 0) ^ lax.broadcasted_iota(jnp.int32, wide, 1)
    for k in range(CHUNK_WINS):
        rows = slice(CELL * k, CELL * (k + 1))
        keep = (apart & cuts_ref[(layer * chunks + chunk) * CHUNK_WINS + k]) == 0
        mixed = []
        for g in range(2):
            q = qkv_out[0, rows, 128 * g : 128 * g + 256]
            key = qkv_out[0, rows, D + 128 * g : D + 128 * g + 256]
            val = qkv_out[0, rows, 2 * D + 128 * g : 2 * D + 128 * g + 256]
            q_wide = jnp.concatenate([q] * GROUP, axis=0) * wide_heads_ref[g]
            lanes = slice(GROUP * CELL * g, GROUP * CELL * (g + 1))
            s = dot_nt(key, q_wide) * SCALE + bias_s[layer, :, lanes]
            s = jnp.where(keep, s, MASKED)
            e = jnp.exp(s - jnp.max(s, axis=0, keepdims=True))
            prob = (e * (1.0 / jnp.sum(e, axis=0, keepdims=True))).astype(bf16)
            prob_out[0, rows, lanes] = prob
            mixed.append(gather_heads(dot_tn(prob, val), heads_ref, g))
        att_out[0, rows, :] = join_groups(*mixed).astype(bf16)
    mid = x + (dot_nn(att_out[0], proj_s[layer]) + vec_out[layer, 2:3, :])
    mid_out[0] = mid
    normal, _ = norm_parts(mid)
    hidden = (normal * vec_out[layer, 5:6, :] + vec_out[layer, 7:8, :]).astype(bf16)
    u = dot_nn(hidden, fc1_s[layer]) + fc1_b[layer]
    cdf = 0.5 * (1.0 + lax.erf(u * ROOT_HALF))
    act_out[0] = (u * cdf).astype(bf16)
    slope_out[0] = (cdf + u * (jnp.exp(-0.5 * u * u) * INV_ROOT_TAU)).astype(bf16)
    y_s[here, :] = mid + (dot_nn(act_out[0], fc2_s[layer]) + vec_out[layer, 3:4, :])

    @pl.when(step == chunks // 2 - 1)
    def _():
        pack_edge(0, y_s, 0, 0)
        edge_copy(0, n_row - 1).start()

    @pl.when(step == chunks + chunks // 2 - 1)
    def _():
        pack_edge(1, y_s, last_row, 2)
        edge_copy(1, 1).start()

    @pl.when(step == 2 * chunks - 1)
    def _():
        edge_copy(2, n_row - 1).wait_recv()
        assemble_ahead(c_s, edge_in.at[2], up_out)
        edge_copy(1, 1).wait_recv()
        assemble_back(y_s, edge_in.at[1], c_s)
        for c in range(chunks):
            rows = slice(CHUNK * c, CHUNK * (c + 1))
            spots = lax.broadcasted_iota(jnp.int32, (CHUNK, tokens), 0) + CHUNK * c
            pick = jnp.where(spots == place_row[...], 1.0, 0.0).astype(bf16)
            rows_out[rows, :] = dot_nn(pick, c_s[...]).astype(bf16)
        for l in range(2):
            end_weights(l)
        for which in range(3):
            edge_copy(which, 1 if which == 1 else n_row - 1).wait_send()
        for w in range(4):
            pltpu.make_async_copy(kept[w], outs[w], out_sem.at[w]).wait()
        if swap:
            swap_end(place, x_in, x_got, x_sem)
            swap_end(place, c_in, c_got, c_sem)


def gather_heads(spread, heads_ref, g):
    total = None
    for h in range(GROUP):
        part = spread[CELL * h : CELL * (h + 1), :] * heads_ref[
            GROUP * g + h : GROUP * g + h + 1, 128 * g : 128 * g + 256
        ]
        total = part if total is None else total + part
    return total


def join_groups(low, high):
    return jnp.concatenate([low[:, :128], low[:, 128:] + high[:, :128], high[:, 128:]], axis=1)


def forward_layers(cuts, placing, x_in, c_in, shards, vectors, rel_table):
    n_row, n_far = lax.axis_size("row"), lax.axis_size("clip") // 2
    tokens = x_in.shape[0]
    chunks = tokens // CHUNK
    swap = can_swap(tokens, n_row * n_far * 2)
    heads, wide = head_masks()
    lanes, order, _ = table_constants()
    table = jnp.pad(rel_table.transpose(0, 2, 1), ((0, 0), (0, 0), (0, TABLE_PAD - TABLE)))
    ff = shards[2].shape[2]
    anywhere = pl.BlockSpec(memory_space=pl.ANY)
    patches = anywhere if swap else whole((tokens, D))
    constants = (
        table,
        jnp.asarray(lanes.reshape(2 * TABLE_PAD, 128), dtype=bf16),
        jnp.asarray(order, dtype=bf16),
        jnp.asarray(heads),
        jnp.asarray(wide, dtype=bf16),
    )
    full = [(2, shard.shape[1] * n_row, shard.shape[2]) for shard in shards]

    def block(i):
        layer = i // chunks
        return layer, (i + layer * (chunks // 2)) % chunks, 0

    saved = [(D, f32), (3 * D, bf16), (HEADS * CELL, bf16), (D, bf16), (D, f32), (ff, bf16), (ff, bf16)]
    dma = pltpu.SemaphoreType.DMA
    n = n_row * n_far * 2
    results = pl.pallas_call(
        functools.partial(forward_kernel, n_row, n_far, swap),
        grid=(2 * chunks,),
        in_specs=[
            pl.BlockSpec(memory_space=pltpu.SMEM),
            whole((tokens, 1)),
            whole((1, tokens)),
            patches,
            patches,
        ]
        + [anywhere] * 5
        + [whole(constant.shape) for constant in constants],
        out_specs=[pl.BlockSpec((1, CHUNK, width), block) for width, _ in saved]
        + [whole((tokens, D))] * 2
        + [anywhere] * 4
        + [whole((2, 8, D))],
        out_shape=[jax.ShapeDtypeStruct((2, tokens, width), kind) for width, kind in saved]
        + [jax.ShapeDtypeStruct((tokens, D), bf16)] * 2
        + [jax.ShapeDtypeStruct(shape, bf16) for shape in full]
        + [jax.ShapeDtypeStruct((2, 8, D), f32)],
        scratch_shapes=[
            pltpu.VMEM((tokens if swap else 16, D), bf16),
            pltpu.VMEM((tokens if swap else 16, D), bf16),
            *[pltpu.VMEM(shape, bf16) for shape in full],
            pltpu.VMEM((n_row, *vectors.shape), bf16),
            pltpu.VMEM((2, 1, 3 * D), f32),
            pltpu.VMEM((2, 1, ff), f32),
            pltpu.VMEM((2, CELL, HEADS * CELL), f32),
            pltpu.VMEM((HEADS // 2 * CELL, 2 * TABLE_PAD), f32),
            pltpu.VMEM((tokens, D), f32),
            pltpu.VMEM((tokens, D), f32),
            pltpu.VMEM((tokens, D), bf16),
            pltpu.VMEM((3, WIN_COLS * 2 * BLOCK, D), bf16),
            pltpu.VMEM((3, WIN_COLS * 2 * BLOCK, D), bf16),
            dma((2, n if swap else 1)),
            dma((2, n if swap else 1)),
            dma((2, 4)),
            dma((2, 2, 3, n_row - 1)),
            dma((2, 2, 3, n_row - 1)),
            dma((2, n_row - 1)),
            dma((2, 3)),
            dma((5,)),
        ],
        compiler_params=pltpu.CompilerParams(
            collective_id=0, has_side_effects=True, vmem_limit_bytes=VMEM_LIMIT
        ),
        name="forward_layers",
    )(cuts, placing.reshape(tokens, 1), placing.reshape(1, tokens), x_in, c_in, *shards, vectors, *constants)
    return results[:7], results[7], results[8], results[9:13], results[13]


BATCHES = ((1, 0), (1, 1), (0, 0), (0, 1))


def batch_rows(n_row, kind):
    return 4 * row_share(n_row) if kind == 0 else 2 * row_share(n_row) + 16


def piece_rows(n_row, n_far, kind):
    return -(-batch_rows(n_row, kind) // (16 * n_far)) * 16


def backward_kernel(
    n_row,
    n_far,
    swap,
    place_row,
    up_ref,
    rows_in,
    x_ref,
    qkv_ref,
    prob_ref,
    att_ref,
    mid_ref,
    act_ref,
    slope_ref,
    qkv_w,
    proj_w,
    fc1_w,
    fc2_w,
    vec_ref,
    heads_ref,
    wide_heads_ref,
    lanes_ref,
    back_ref,
    rows_out,
    grad_out,
    final_m_out,
    final_a_out,
    vec_g,
    fc1_bg,
    table_g,
    g_s,
    h1_s,
    dt_s,
    ga_s,
    h2_s,
    du_s,
    gz_s,
    grad_rows,
    edge_out,
    edge_in,
    pack_m,
    pack_a,
    got_am,
    got_aa,
    got_bm,
    got_ba,
    out_cm,
    out_ca,
    got_cm,
    got_ca,
    final_m,
    final_a,
    rows_sem,
    grad_sem,
    edge_sem,
    a_sem,
    b_sem,
    c_sem,
    d_sem,
    e_sem,
    done_sem,
):
    step = pl.program_id(0)
    tokens = g_s.shape[1]
    chunks = tokens // CHUNK
    layer = 1 - step // (2 * chunks)
    kind = step // chunks % 2
    chunk = (step + chunks // 2) % chunks
    place = Place(n_row, n_far)
    core, row, far = place.core, place.row, place.far
    size = row_share(n_row)
    last_row = (tokens // CELL // WIN_COLS - 1) * WIN_COLS
    packs, got_as, got_bs = (pack_m, pack_a), (got_am, got_aa), (got_bm, got_ba)
    out_cs, got_cs, finals = (out_cm, out_ca), (got_cm, got_ca), (final_m, final_a)
    here = pl.ds(pl.multiple_of(chunk * CHUNK, CHUNK), CHUNK)

    def edge_copy():
        return remote(
            edge_out, edge_in, edge_sem.at[0], edge_sem.at[1], place.in_row(1)
        )

    def part(ref, b, at):
        rows = got_cs[BATCHES[b][1]].shape[2]
        return ref.at[BATCHES[b][0], pl.ds(pl.multiple_of(at * rows, 16), rows), :]

    def copy_a(b):
        l, k = BATCHES[b]
        return remote(
            packs[k].at[l, 1 - core], got_as[k].at[l], a_sem.at[0, b], a_sem.at[1, b], place.twin()
        )

    def copy_b(b, d):
        l, k = BATCHES[b]
        return remote(
            packs[k].at[l, core, place.row_at(d)],
            got_bs[k].at[l, d - 1],
            b_sem.at[0, b, d - 1],
            b_sem.at[1, b, d - 1],
            place.in_row(d),
        )

    def copy_c(b, d):
        l, k = BATCHES[b]
        return remote(
            part(out_cs[k], b, place.far_at(d)),
            got_cs[k].at[l, d - 1],
            c_sem.at[0, b, d - 1],
            c_sem.at[1, b, d - 1],
            place.along(d),
        )

    def copy_d(b, d, owner):
        spot = part(finals[BATCHES[b][1]].at[core], b, owner)
        return remote(
            spot, spot, d_sem.at[0, b, d - 1], d_sem.at[1, b, d - 1], place.along(d)
        )

    def copy_e(b, d, half):
        spot = part(finals[BATCHES[b][1]].at[half], b, place.far_at((n_far - d) % n_far))
        return remote(spot, spot, e_sem.at[0, b, d], e_sem.at[1, b, d], place.twin())

    def sum_cores(b):
        l, k = BATCHES[b]
        copy_a(b).wait_recv()
        for d in range(1, n_row):
            r = place.row_at(d)
            packs[k][l, core, r] = packs[k][l, core, r] + got_as[k][l, r]
            copy_b(b, d).start()
        packs[k][l, core, row] = packs[k][l, core, row] + got_as[k][l, row]

    def sum_row(b):
        l, k = BATCHES[b]
        total = packs[k][l, core, row].astype(f32)
        for d in range(1, n_row):
            copy_b(b, d).wait_recv()
            total += got_bs[k][l, d - 1].astype(f32)
        out_cs[k][l, 0 : batch_rows(n_row, k), :] = total.astype(bf16)
        for d in range(1, n_far):
            copy_c(b, d).start()

    def sum_far(b):
        l, k = BATCHES[b]
        total = part(out_cs[k], b, far)[...].astype(f32)
        for d in range(1, n_far):
            copy_c(b, d).wait_recv()
            total += got_cs[k][l, d - 1].astype(f32)
        part(finals[k].at[core], b, far)[...] = total.astype(bf16)
        for d in range(1, n_far):
            copy_d(b, d, far).start()
        copy_e(b, 0, core).start()

    def pass_on(b):
        for d in range(1, n_far):
            copy_d(b, d, place.far_at(n_far - d)).wait_recv()
            copy_e(b, d, core).start()

    def finish(b):
        copy_a(b).wait_send()
        for d in range(1, n_row):
            copy_b(b, d).wait_send()
        for d in range(1, n_far):
            copy_c(b, d).wait_send()
            copy_d(b, d, far).wait_send()
        for d in range(n_far):
            copy_e(b, d, core).wait_send()
            copy_e(b, d, 1 - core).wait_recv()

    @pl.when(step == 0)
    def _():
        if swap:
            swap_own(place, rows_in, rows_out, rows_sem).start()
            meet_all(place)
            swap_start(place, rows_in, rows_out, rows_sem)
        else:
            pltpu.make_async_copy(rows_in, rows_out, rows_sem.at[0, 0]).start()
            meet(place.partners())
        g_s[1] = up_ref[...].astype(f32)
        for k in range(2):
            valid, padded = batch_rows(n_row, k), out_cs[k].shape[1]
            if padded > valid:
                out_cs[k][:, valid:, :] = jnp.zeros((2, padded - valid, D), bf16)

    @pl.when(step == chunks + 1)
    def _():
        sum_cores(0)

    @pl.when(step == 2 * chunks)
    def _():
        edge_copy().wait_recv()
        assemble_back(g_s.at[1], edge_in, g_s.at[0])
        sum_row(0)

    @pl.when(step == 2 * chunks + 1)
    def _():
        sum_cores(1)

    @pl.when(step == 2 * chunks + 2)
    def _():
        sum_far(0)

    @pl.when(step == 3 * chunks - 1)
    def _():
        sum_row(1)
        pass_on(0)

    @pl.when(step == 3 * chunks)
    def _():
        sum_far(1)

    @pl.when(step == 3 * chunks + 1)
    def _():
        sum_cores(2)
        pass_on(1)

    @pl.when(step % (2 * chunks) == 0)
    def _():
        vec_g[...] = jnp.zeros_like(vec_g)
        fc1_bg[...] = jnp.zeros_like(fc1_bg)
        table_g[...] = jnp.zeros_like(table_g)

    @pl.when(kind == 0)
    def _():
        upstream = g_s[layer, here, :]
        low = upstream.astype(bf16)
        gz_s[here, :] = low
        vec_g[3:4, :] += column_sum(low.astype(f32))
        du = (dot_nt(low, fc2_w[0]) * slope_ref[0].astype(f32)).astype(bf16)
        du_s[here, :] = du
        fc1_bg[...] += column_sum(du.astype(f32))
        dn = dot_nt(du, fc1_w[0])
        normal, inverse = norm_parts(mid_ref[0])
        gain = vec_ref[layer, 5:6, :]
        h2_s[here, :] = (normal * gain + vec_ref[layer, 7:8, :]).astype(bf16)
        vec_g[5:6, :] += column_sum(dn * normal)
        vec_g[7:8, :] += column_sum(dn)
        mid_grad = upstream + norm_back(dn, normal, inverse, gain)
        g_s[layer, here, :] = mid_grad
        low = mid_grad.astype(bf16)
        ga_s[here, :] = low
        vec_g[2:3, :] += column_sum(low.astype(f32))

    @pl.when(step % (2 * chunks) == chunks - 1)
    def _():
        for j in range(4):
            lanes = slice(D * j, D * (j + 1))
            value = dot_tn(h2_s[...], du_s[:, lanes]).astype(bf16)
            for r in range(n_row):
                pack_m[layer, 0, r, size * j : size * (j + 1), :] = value[
                    size * r : size * (r + 1), :
                ]
            value = dot_tn(act_ref[0, :, lanes], gz_s[...]).astype(bf16)
            count = D // (4 * size)
            for t in range(count):
                pack_m[layer, 1, j * count + t] = value[4 * size * t : 4 * size * (t + 1), :]

    @pl.when(step == chunks - 1)
    def _():
        copy_a(0).start()

    @pl.when(step == 3 * chunks - 1)
    def _():
        copy_a(2).start()

    @pl.when(kind == 1)
    def _():
        att_grad = dot_nt(ga_s[here, :], proj_w[0]).astype(bf16)
        for k in range(CHUNK_WINS):
            rows = slice(CELL * k, CELL * (k + 1))
            there = pl.ds(pl.multiple_of(chunk * CHUNK + CELL * k, CELL), CELL)
            q_parts, k_parts, v_parts = [], [], []
            for g in range(2):
                q = qkv_ref[0, rows, 128 * g : 128 * g + 256]
                key = qkv_ref[0, rows, D + 128 * g : D + 128 * g + 256]
                val = qkv_ref[0, rows, 2 * D + 128 * g : 2 * D + 128 * g + 256]
                do = att_grad[rows, 128 * g : 128 * g + 256]
                q_wide = jnp.concatenate([q] * GROUP, axis=0) * wide_heads_ref[g]
                do_wide = jnp.concatenate([do] * GROUP, axis=0) * wide_heads_ref[g]
                lanes = slice(GROUP * CELL * g, GROUP * CELL * (g + 1))
                prob_low = prob_ref[0, rows, lanes]
                prob = prob_low.astype(f32)
                dp = dot_nt(val, do_wide)
                v_parts.append(dot_nn(prob_low, do_wide))
                weighted = prob * dp
                ds = (weighted - prob * column_sum(weighted)).astype(bf16)
                table_g[:, lanes] += ds.astype(f32)
                k_parts.append(dot_nn(ds, q_wide))
                q_parts.append(gather_heads(dot_tn(ds, key), heads_ref, g))
            dt_s[there, 0:D] = (join_groups(*q_parts) * SCALE).astype(bf16)
            dt_s[there, D : 2 * D] = (join_groups(*k_parts) * SCALE).astype(bf16)
            dt_s[there, 2 * D : 3 * D] = join_groups(*v_parts).astype(bf16)
        dt = dt_s[here, :]
        vec_g[0:1, :] += column_sum(dt[:, 0:D].astype(f32))
        vec_g[1:2, :] += column_sum(dt[:, 2 * D :].astype(f32))
        dn = dot_nt(dt, qkv_w[0])
        normal, inverse = norm_parts(x_ref[0])
        gain = vec_ref[layer, 4:5, :]
        h1_s[here, :] = (normal * gain + vec_ref[layer, 6:7, :]).astype(bf16)
        vec_g[4:5, :] += column_sum(dn * normal)
        vec_g[6:7, :] += column_sum(dn)
        g_s[layer, here, :] += norm_back(dn, normal, inverse, gain)

    @pl.when(step == chunks + chunks // 2 - 1)
    def _():
        for col in range(WIN_COLS):
            at = CELL * (last_row + col) + 2 * BLOCK
            edge_out[2 * BLOCK * col : 2 * BLOCK * (col + 1), :] = g_s[
                1, at : at + 2 * BLOCK, :
            ].astype(bf16)
        edge_copy().start()

    @pl.when(step == 4 * chunks - 1)
    def _():
        source = g_s[0].astype(bf16)
        for c in range(chunks):
            rows = slice(CHUNK * c, CHUNK * (c + 1))
            spots = lax.broadcasted_iota(jnp.int32, (CHUNK, tokens), 0) + CHUNK * c
            pick = jnp.where(spots == place_row[...], 1.0, 0.0).astype(bf16)
            grad_rows[rows, :] = dot_nn(pick, source).astype(bf16)
        if swap:
            swap_own(place, grad_rows, grad_out, grad_sem).start()
            swap_start(place, grad_rows, grad_out, grad_sem)
        else:
            pltpu.make_async_copy(grad_rows, grad_out, grad_sem.at[0, 0]).start()

    @pl.when(step % (2 * chunks) == 2 * chunks - 1)
    def _():
        def put(half, at, value):
            for r in range(n_row):
                pack_a[layer, half, r, at : at + size, :] = value[size * r : size * (r + 1), :]

        for j in range(3):
            value = dot_tn(h1_s[...], dt_s[:, D * j : D * (j + 1)]).astype(bf16)
            put(j // 2, size * (j % 2), value)
        put(1, size, dot_tn(att_ref[0], ga_s[...]).astype(bf16))
        table = table_rows(table_g[...], lanes_ref, back_ref)
        table = jnp.concatenate([table, jnp.zeros((HEADS, D - TABLE_PAD), f32)], axis=1)
        vectors = jnp.concatenate(
            [vec_g[...]]
            + [fc1_bg[:, D * j : D * (j + 1)] for j in range(4)]
            + [jnp.zeros((4, D), f32)],
            axis=0,
        )
        for r in range(n_row):
            pack_a[layer, 0, r, 2 * size :, :] = vectors.astype(bf16)
            pack_a[layer, 1, r, 2 * size :, :] = table.astype(bf16)

    @pl.when(step == 2 * chunks - 1)
    def _():
        copy_a(1).start()

    @pl.when(step == 4 * chunks - 1)
    def _():
        copy_a(3).start()
        sum_row(2)
        sum_cores(3)
        sum_far(2)
        sum_row(3)
        pass_on(2)
        sum_far(3)
        pass_on(3)
        for b in range(4):
            finish(b)
        edge_copy().wait_send()
        copies = [
            pltpu.make_async_copy(final_m, final_m_out, done_sem.at[0]),
            pltpu.make_async_copy(final_a, final_a_out, done_sem.at[1]),
        ]
        for copy in copies:
            copy.start()
        for copy in copies:
            copy.wait()
        for source, target, sem in (
            (rows_in, rows_out, rows_sem),
            (grad_rows, grad_out, grad_sem),
        ):
            if swap:
                swap_wait(place, source, target, sem)
                swap_end(place, source, target, sem)
                swap_own(place, source, target, sem).wait()
            else:
                pltpu.make_async_copy(source, target, sem.at[0, 0]).wait()


def backward_layers(placing, upstream, rows, saved, full, vec):
    n_row, n_far = lax.axis_size("row"), lax.axis_size("clip") // 2
    n = 2 * n_row * n_far
    tokens = upstream.shape[0]
    chunks = tokens // CHUNK
    swap = can_swap(tokens, n)
    heads, wide = head_masks()
    lanes, _, back = table_constants()
    ff = full[2].shape[2]
    size = row_share(n_row)
    anywhere = pl.BlockSpec(memory_space=pl.ANY)

    def at(i):
        return 1 - i // (2 * chunks), i // chunks % 2, (i + chunks // 2) % chunks

    def layer_block(i):
        return 1 - i // (2 * chunks), 0, 0

    def forward_block(i):
        layer, kind, chunk = at(i)
        return (1 - kind) * layer, (1 - kind) * chunk + kind * (chunks // 2 - 1 + layer), 0

    def attention_block(i):
        layer, kind, chunk = at(i)
        return layer, kind * chunk + (1 - kind) * (chunks // 2), 0

    def chunked(value, block):
        return pl.BlockSpec((1, CHUNK, value.shape[2]), block)

    def layered(value):
        return pl.BlockSpec((1, *value.shape[1:]), layer_block)

    x, qkv, prob, att, mid, act, slope = saved
    constants = (
        vec,
        jnp.asarray(heads),
        jnp.asarray(wide, dtype=bf16),
        jnp.asarray(lanes.reshape(2 * TABLE_PAD, 128), dtype=bf16),
        jnp.asarray(back, dtype=bf16),
    )
    valid = [batch_rows(n_row, k) for k in range(2)]
    piece = [piece_rows(n_row, n_far, k) for k in range(2)]
    final = [(2, 2, n_far * piece[k], D) for k in range(2)]
    dma = pltpu.SemaphoreType.DMA

    def pair(shape_of):
        return [pltpu.VMEM(shape_of(k), bf16) for k in range(2)]

    return pl.pallas_call(
        functools.partial(backward_kernel, n_row, n_far, swap),
        grid=(4 * chunks,),
        in_specs=[
            whole((1, tokens)),
            whole((tokens, D)),
            anywhere,
            chunked(x, attention_block),
            chunked(qkv, attention_block),
            chunked(prob, attention_block),
            layered(att),
            chunked(mid, forward_block),
            layered(act),
            chunked(slope, forward_block),
        ]
        + [layered(weight) for weight in full]
        + [whole(constant.shape) for constant in constants],
        out_specs=[anywhere] * 4,
        out_shape=[jax.ShapeDtypeStruct((tokens, D), bf16)] * 2
        + [jax.ShapeDtypeStruct(shape, bf16) for shape in final],
        scratch_shapes=[
            pltpu.VMEM((8, D), f32),
            pltpu.VMEM((1, ff), f32),
            pltpu.VMEM((CELL, HEADS * CELL), f32),
            pltpu.VMEM((2, tokens, D), f32),
            pltpu.VMEM((tokens, D), bf16),
            pltpu.VMEM((tokens, 3 * D), bf16),
            pltpu.VMEM((tokens, D), bf16),
            pltpu.VMEM((tokens, D), bf16),
            pltpu.VMEM((tokens, ff), bf16),
            pltpu.VMEM((tokens, D), bf16),
            pltpu.VMEM((tokens, D), bf16),
            pltpu.VMEM((WIN_COLS * 2 * BLOCK, D), bf16),
            pltpu.VMEM((WIN_COLS * 2 * BLOCK, D), bf16),
            *pair(lambda k: (2, 2, n_row, valid[k], D)),
            *pair(lambda k: (2, n_row, valid[k], D)),
            *pair(lambda k: (2, n_row - 1, valid[k], D)),
            *pair(lambda k: (2, n_far * piece[k], D)),
            *pair(lambda k: (2, n_far - 1, piece[k], D)),
            *pair(lambda k: final[k]),
            dma((2, n if swap else 1)),
            dma((2, n if swap else 1)),
            dma((2,)),
            dma((2, 4)),
            dma((2, 4, n_row - 1)),
            dma((2, 4, n_far - 1)),
            dma((2, 4, n_far - 1)),
            dma((2, 4, n_far)),
            dma((2,)),
        ],
        compiler_params=pltpu.CompilerParams(
            collective_id=1, has_side_effects=True, vmem_limit_bytes=VMEM_LIMIT
        ),
        name="backward_layers",
    )(placing.reshape(1, tokens), upstream, rows, x, qkv, prob, att, mid, act, slope, *full, *constants)


def unpack_kernel(
    n_row, m_ref, a_ref, qkv_o, qvb_o, proj_o, projb_o, fc1_o, fc1b_o, fc2_o, fc2b_o, gain_o, shift_o, table_o
):
    row = lax.axis_index("row")
    size = D // n_row
    lane = lax.broadcasted_iota(jnp.int32, (D, size), 0)
    want = lax.broadcasted_iota(jnp.int32, (D, size), 1)
    pick = jnp.where(lane == want + size * row, 1.0, 0.0).astype(bf16)
    start = 4 * size * row
    lane = lax.broadcasted_iota(jnp.int32, (D, 4 * size), 0)
    want = lax.broadcasted_iota(jnp.int32, (D, 4 * size), 1)
    pick_fc1 = jnp.where(lane == want + start % D, 1.0, 0.0).astype(bf16)
    spot = lax.broadcasted_iota(jnp.int32, (16, 4 * size), 0)
    a = lax.broadcasted_iota(jnp.int32, (HEADS, HEADS), 0)
    b = lax.broadcasted_iota(jnp.int32, (HEADS, HEADS), 1)
    same = jnp.where(a == b, 1.0, 0.0).astype(bf16)
    for layer in range(2):
        for j in range(3):
            at = size * (j % 2)
            qkv_o[layer, :, D * j : D * (j + 1)] = a_ref[j // 2, layer, at : at + size, :].astype(f32)
        proj_o[layer] = a_ref[1, layer, size : 2 * size, :].astype(f32)
        for j in range(4):
            fc1_o[layer, :, D * j : D * (j + 1)] = m_ref[
                0, layer, size * j : size * (j + 1), :
            ].astype(f32)
        fc2_o[layer] = m_ref[1, layer, 0 : 4 * size, :].astype(f32)
        vectors = a_ref[0, layer, 2 * size : 2 * size + 16, :]
        mine = dot_nn(vectors, pick)
        qvb_o[layer] = mine[0:2]
        projb_o[layer : layer + 1] = mine[2:3]
        fc2b_o[layer : layer + 1] = mine[3:4]
        gain_o[layer] = mine[4:6]
        shift_o[layer] = mine[6:8]
        mine = dot_nn(vectors, pick_fc1)
        fc1b_o[layer : layer + 1] = column_sum(jnp.where(spot == 8 + start // D, mine, 0.0))
        table = a_ref[1, layer, 2 * size : 2 * size + 16, 0:TABLE_PAD]
        table_o[layer] = dot_tn(table, same)[0:TABLE, :]


def unpack_gradients(final_m, final_a):
    n_row = lax.axis_size("row")
    size = D // n_row
    shapes = [
        (2, size, 3 * D),
        (2, 2, size),
        (2, size, D),
        (2, size),
        (2, size, 4 * D),
        (2, 4 * size),
        (2, 4 * size, D),
        (2, size),
        (2, 2, size),
        (2, 2, size),
        (2, TABLE, HEADS),
    ]
    return pl.pallas_call(
        functools.partial(unpack_kernel, n_row),
        out_shape=[jax.ShapeDtypeStruct(shape, f32) for shape in shapes],
        compiler_params=pltpu.CompilerParams(vmem_limit_bytes=VMEM_LIMIT),
        name="unpack_gradients",
    )(final_m, final_a)


def exchange(values):
    return lax.all_to_all(values, ("clip", "row"), split_axis=0, concat_axis=0, tiled=True)


def body(
    inputs,
    cotangent,
    source_of,
    split_row,
    qkv_weight,
    qv_bias,
    proj_weight,
    proj_bias,
    fc1_weight,
    fc1_bias,
    fc2_weight,
    fc2_bias,
    norm_gain,
    norm_bias,
    rel_table,
):
    clip_count = lax.axis_size("clip")
    row_count = lax.axis_size("row")
    tokens = inputs.shape[0]
    block_rows = tokens // (clip_count * row_count)
    grid_rows = tokens // GRID_COLS
    slot_rows = grid_rows * row_count
    window_rows = grid_rows // WIN
    part = D // row_count

    placing = source_of // tokens * block_rows + source_of % block_rows
    placing = placing.reshape(window_rows, 2, SHIFT, WIN_COLS, 2, SHIFT)
    placing = placing.transpose(0, 3, 1, 4, 2, 5).reshape(tokens)
    middle = lax.axis_index("row") * grid_rows + WIN * (1 + jnp.arange(window_rows))
    row_cut = ((middle == split_row[0]) | (middle == slot_rows)).astype(jnp.int32)
    col_cut = (jnp.arange(WIN_COLS) == WIN_COLS - 1).astype(jnp.int32)
    cuts = (32 * row_cut[:, None] + 16 * col_cut[None, :]).reshape(-1)

    cuts = jnp.concatenate([jnp.zeros_like(cuts), cuts])

    vectors = jnp.concatenate(
        [qv_bias, proj_bias[:, None], fc2_bias[:, None], norm_gain, norm_bias], axis=1
    )
    vectors = jnp.concatenate(
        [
            jnp.pad(vectors, ((0, 0), (0, 0), (0, D - part))),
            jnp.pad(fc1_bias[:, None], ((0, 0), (0, 7), (0, D - 4 * part))),
        ],
        axis=1,
    ).reshape(32, D)
    if not can_swap(tokens, clip_count * row_count):
        inputs, cotangent = exchange(inputs), exchange(cotangent)
    saved, upstream, out_rows, full, vec_rows = forward_layers(
        cuts,
        placing,
        inputs,
        cotangent,
        (qkv_weight, proj_weight, fc1_weight, fc2_weight),
        vectors,
        rel_table,
    )
    output, input_grad, *finals = backward_layers(placing, upstream, out_rows, saved, full, vec_rows)
    if not can_swap(tokens, clip_count * row_count):
        output, input_grad = exchange(output), exchange(input_grad)
    input_grad = input_grad.astype(f32)
    totals = unpack_gradients(*finals)
    return (output, input_grad, *totals)


def solution(mesh):
    placed = (
        P(("clip", "row"), None),
        P(("clip", "row"), None),
        P(("clip", "row")),
        P("clip"),
        P(None, "row", None),
        P(None, None, "row"),
        P(None, "row", None),
        P(None, "row"),
        P(None, "row", None),
        P(None, "row"),
        P(None, "row", None),
        P(None, "row"),
        P(None, None, "row"),
        P(None, None, "row"),
        P(),
    )
    return jax.shard_map(
        body,
        mesh=mesh,
        in_specs=placed,
        out_specs=(
            P(("clip", "row"), None),
            P(("clip", "row"), None),
            P(None, "row", None),
            P(None, None, "row"),
            P(None, "row", None),
            P(None, "row"),
            P(None, "row", None),
            P(None, "row"),
            P(None, "row", None),
            P(None, "row"),
            P(None, None, "row"),
            P(None, None, "row"),
            P(),
        ),
        check_vma=False,
    )
```

profile of v0, /device:TPU:0, one launch (start us, length us, event | category | flops | bytes accessed | tf_op | source)
XLA Modules:
  0.0 249.5 jit_solution(9343432234641020107)
XLA Ops:
  1.3 0.1 broadcast_add_fusion
  1.4 0.1 add.60
  1.5 0.6 concatenate.9.cuts_ref
  2.1 0.7 fusion.3
  2.8 0.7 constant_dynamic-update-slice_fusion.4
  3.4 0.7 constant_dynamic-update-slice_fusion.3
  4.1 0.7 constant_dynamic-update-slice_fusion.2
  4.8 0.7 constant_dynamic-update-slice_fusion.1
  5.5 0.7 constant_dynamic-update-slice_fusion
  6.1 0.7 fusion
  6.8 0.6 copy.42
  7.5 1.4 pad.15.table_ref
  8.8 0.2 reshape.53
  9.1 0.1 copy.37
  9.1 0.8 reshape_reshape.7.place_row
  9.9 1.0 reshape_reshape.9.place_col
  10.9 103.8 %forward_layers.1 = (f32[2,1024,384]{2,1,0:T(8,128)}, bf16[2,1024,1152]{2,1,0:T(8,128)(2,1)}, bf16[2,1024,1024]{2,1,0:T(8,128)(2,1)}, bf16[2,1024,384]{2,1,0:T(8...) custom-call(s32[32]{0:T(128)} %concatenate.9.cuts_ref, ...), custom_call_target="tpu_custom_call" | custom-call | tf_op jit(solution)/shard_map/forward_layers/pallas_call | solution.py:670
  114.7 126.1 %backward_layers.1 = (bf16[1024,384]{1,0:T(8,128)(2,1)}, bf16[1024,384]{1,0:T(8,128)(2,1)}, bf16[2,2,384,384]{3,2,1,0:T(8,128)(2,1)}, bf16[2,2,256,384]{3,2,1,0:T(8,128)(2,1)}) custom-call(s32[1,1024]{1,0:T(1,128)} %reshape_reshape.7.place_row, bf16[1024,384]{1,0:T(8,128)(2,1)} %get-tuple-element.42.up_ref, bf16[1024,384]{1,0:T(8,128)(2,1)} %get-tuple-element.43.rows_in, ...), custom_call_target="tpu_custom_call" | custom-call | tf_op jit(solution)/shard_map/backward_layers/pallas_call | solution.py:1163
  240.8 0.0 copy-start
  240.8 2.5 convert_element_type.13
  243.2 3.7 %unpack_gradients.1 = (f32[2,96,1152]{2,1,0:T(8,128)}, f32[2,2,96]{2,1,0:T(2,128)}, f32[2,96,384]{2,1,0:T(8,128)}, f32[2,96]{1,0:T(2,128)}, f32[2,96,1536]{2,1,0...) custom-call(bf16[2,2,384,384]{3,2,1,0:T(8,128)(2,1)} %get-tuple-elem, ...), custom_call_target="tpu_custom_call" | custom-call | tf_op jit(solution)/shard_map/unpack_gradients/pallas_call | solution.py:1275
  247.0 1.7 copy.44
  248.6 0.0 copy-done
  248.6 0.9 copy.54
  (2 shorter events, 0.0 us)
Async XLA Ops:
  240.8 7.8 %copy-start = (bf16[1024,384]{1,0:T(8,128)(2,1)S(1)}, bf16[1024,384]{1,0:T(8,128)(2,1)}, u32[]{:S(2)}) copy-start(bf16[1024,384]{1,0:T(8,128)(2,1)} %get-tuple-element.110) | copy-start | bytes 2359300
where the time goes:
time: 251 us; the launch traced here: 249 us
  Pallas kernels  234 us (93%)
  local copies, waits for them, and re-layouts  10.6 us (4%)
  other arithmetic  3.92 us (2%)
    pallas_call x1, Pallas kernels, backward_layers(): pl.pallas_call(functools.partial(backward_kernel, n_row, n_far, swap), gr...  126 us
    pallas_call x1, Pallas kernels, forward_layers(): pl.pallas_call(functools.partial(forward_kernel, n_row, n_far, swap), gri...  104 us
    unnamed x8, local copies, waits for them, and re-layouts  5.24 us

commit v1 on v0

--- a/solution.py
+++ b/solution.py
@@ -177,22 +177,22 @@
             out_ref[quarter(window, sub), :] = value.astype(out_ref.dtype)
 
 
-def assemble_ahead(main_ref, edge_ref, out_ref):
-    windows = main_ref.shape[0] // CELL
-    last = windows // WIN_COLS - 1
-    for window in range(windows):
-        wr, wc = divmod(window, WIN_COLS)
-        after = (wc + 1) % WIN_COLS
-        out_ref[quarter(window, 0), :] = main_ref[quarter(window, 3), :].astype(out_ref.dtype)
-        out_ref[quarter(window, 1), :] = main_ref[
-            quarter(wr * WIN_COLS + after, 2), :
-        ].astype(out_ref.dtype)
-        for sub, col, piece in ((2, wc, 1), (3, after, 0)):
-            if wr == last:
-                value = edge_ref[pl.ds(2 * BLOCK * col + BLOCK * piece, BLOCK), :]
-            else:
-                value = main_ref[quarter((wr + 1) * WIN_COLS + col, piece), :]
-            out_ref[quarter(window, sub), :] = value.astype(out_ref.dtype)
+def assemble_ahead(main_ref, edge_ref, out_ref, window_rows):
+    last = main_ref.shape[0] // CELL // WIN_COLS - 1
+    for wr in window_rows:
+        for wc in range(WIN_COLS):
+            window = wr * WIN_COLS + wc
+            after = (wc + 1) % WIN_COLS
+            out_ref[quarter(window, 0), :] = main_ref[quarter(window, 3), :].astype(out_ref.dtype)
+            out_ref[quarter(window, 1), :] = main_ref[
+                quarter(wr * WIN_COLS + after, 2), :
+            ].astype(out_ref.dtype)
+            for sub, col, piece in ((2, wc, 1), (3, after, 0)):
+                if wr == last:
+                    value = edge_ref[pl.ds(2 * BLOCK * col + BLOCK * piece, BLOCK), :]
+                else:
+                    value = main_ref[quarter((wr + 1) * WIN_COLS + col, piece), :]
+                out_ref[quarter(window, sub), :] = value.astype(out_ref.dtype)
 
 
 class Place:
@@ -219,11 +219,17 @@
     def twin(self):
         return (2 * self.far + 1 - self.core, self.row)
 
+    def at_row(self, row):
+        return (2 * self.far + self.core, row)
+
     def in_row(self, d):
-        return (2 * self.far + self.core, self.row_at(d))
+        return self.at_row(self.row_at(d))
+
+    def at_far(self, far):
+        return (2 * far + self.core, self.row)
 
     def along(self, d):
-        return (2 * self.far_at(d) + self.core, self.row)
+        return self.at_far(self.far_at(d))
 
     def partners(self, far=True):
         found = [self.twin()] + [self.in_row(d) for d in range(1, self.n_row)]
@@ -325,15 +331,20 @@
     return D // n_row
 
 
-HALVES = (((0, 0, 1), (1, 0, 1), (3, 0, 2)), ((2, 0, 1), (3, 2, 2)))
 HEIGHTS = (1, 1, 1, 4)
+KINDS = ((0, 1), (2, 3))
+
+
+def shard_half(height, core):
+    low = -(-height // 32) * 16
+    return (0, low) if core == 0 else (low, height - low)
 
 
 def forward_kernel(
     n_row,
     n_far,
     swap,
-    cuts_ref,
+    split_ref,
     place_col,
     place_row,
     x_in,
@@ -342,7 +353,12 @@
     proj_i,
     fc1_i,
     fc2_i,
-    vec_i,
+    qv_bias,
+    proj_bias,
+    fc1_bias,
+    fc2_bias,
+    gain_ref,
+    shift_ref,
     table_ref,
     lanes_ref,
     order_ref,
@@ -356,7 +372,7 @@
     act_out,
     slope_out,
     up_out,
-    rows_out,
+    y_out,
     qkv_wo,
     proj_wo,
     fc1_wo,
@@ -368,14 +384,18 @@
     proj_s,
     fc1_s,
     fc2_s,
+    vec_wide,
+    vec_mine,
     vec_got,
     qkv_b,
     fc1_b,
+    table_s,
     bias_s,
     wide_s,
     x_s,
     y_s,
     c_s,
+    order_s,
     edge_out,
     edge_in,
     x_sem,
@@ -390,117 +410,156 @@
     step = pl.program_id(0)
     tokens = x_s.shape[0]
     chunks = tokens // CHUNK
-    layer = step // chunks
-    chunk = (step + layer * (chunks // 2)) % chunks
+    layer = step // (2 * chunks)
+    kind = step // chunks % 2
+    chunk = (step + layer * kind * (chunks // 2)) % chunks
     place = Place(n_row, n_far)
     size = row_share(n_row)
     shards = (qkv_i, proj_i, fc1_i, fc2_i)
     kept = (qkv_s, proj_s, fc1_s, fc2_s)
     outs = (qkv_wo, proj_wo, fc1_wo, fc2_wo)
-    last_row = (tokens // CELL // WIN_COLS - 1) * WIN_COLS
+    window_rows = tokens // CELL // WIN_COLS
+    last_row = (window_rows - 1) * WIN_COLS
+    square = n_row == 4
+    direct = range(2 if square else n_row - 1)
+    slots = range(n_row - 1)
     if not swap:
         x_got, c_got = x_in, c_in
 
     def own(l, w):
         return pltpu.make_async_copy(
-            shards[w].at[l], spot(l, w, place.row, 0, HEIGHTS[w]), own_sem.at[l, w]
+            shards[w].at[l], spot(l, w, place.row, 0, HEIGHTS[w] * size), own_sem.at[l, w]
         )
 
     def spot(l, w, owner, first, count):
-        at = pl.multiple_of((owner * HEIGHTS[w] + first) * size, 16)
-        return kept[w].at[l, pl.ds(at, count * size), :]
-
-    def push(l, core, i, d, source=None):
-        w, first, count = HALVES[core][i]
+        at = pl.multiple_of(owner * HEIGHTS[w] * size + first, 16)
+        return kept[w].at[l, pl.ds(at, count), :]
+
+    def neighbour(slot):
+        row = place.row
+        return (row + 1 - 2 * (row % 2), (row + 2) % 4, 3 - row)[slot]
+
+    def source(slot):
+        return neighbour(slot) if square else place.row_at(n_row - 1 - slot)
+
+    def target(slot):
+        return place.at_row(neighbour(slot) if square else place.row_at(slot + 1))
+
+    def push(l, core, w, slot, owner=None):
+        first, count = shard_half(HEIGHTS[w] * size, core)
         return remote(
-            shards[w].at[l, pl.ds(first * size, count * size), :],
-            spot(l, w, place.row if source is None else source, first, count),
-            row_sem.at[0, l, i, d - 1],
-            row_sem.at[1, l, i, d - 1],
-            place.in_row(d),
+            shards[w].at[l, pl.ds(first, count), :],
+            spot(l, w, place.row if owner is None else owner, first, count),
+            row_sem.at[0, l, w, slot],
+            row_sem.at[1, l, w, slot],
+            target(slot),
         )
 
-    def hand(l, core, i, d):
-        w, first, count = HALVES[core][i]
-        here = spot(l, w, place.row_at(n_row - d), first, count)
+    def relay(l, core, w):
+        axis = (w + core) % 2
+        here = spot(l, w, source(axis), *shard_half(HEIGHTS[w] * size, core))
         return remote(
-            here, here, twin_sem.at[0, l, i, d - 1], twin_sem.at[1, l, i, d - 1], place.twin()
+            here, here, row_sem.at[0, l, w, 2], row_sem.at[1, l, w, 2], target(1 - axis)
         )
 
-    def pieces(core):
-        return [(i, d) for i in range(len(HALVES[core])) for d in range(1, n_row)]
+    def hand(l, core, w, slot):
+        here = spot(l, w, source(slot), *shard_half(HEIGHTS[w] * size, core))
+        return remote(
+            here, here, twin_sem.at[0, l, w, slot], twin_sem.at[1, l, w, slot], place.twin()
+        )
 
     def by_core(work):
         for core in range(2):
             pl.when(place.core == core)(functools.partial(work, core))
 
-    def start_weights(l):
+    def start_weights(l, k):
         def work(core):
-            for i, d in pieces(core):
-                push(l, core, i, d).start()
+            for w in KINDS[k]:
+                for slot in direct:
+                    push(l, core, w, slot).start()
 
         by_core(work)
 
-    def pass_weights(l):
+    def pass_weights(l, k):
         def work(core):
-            for i, d in pieces(core):
-                push(l, core, i, d, place.row_at(n_row - d)).wait_recv()
-                hand(l, core, i, d).start()
+            for w in KINDS[k]:
+                for slot in direct:
+                    push(l, core, w, slot, source(slot)).wait_recv()
+                    if square and slot == (w + core) % 2:
+                        relay(l, core, w).start()
+                    hand(l, core, w, slot).start()
 
         by_core(work)
 
-    def wait_weights(l):
+    def pass_relayed(l, k):
         def work(core):
-            for i, d in pieces(1 - core):
-                hand(l, 1 - core, i, d).wait_recv()
+            for w in KINDS[k]:
+                push(l, core, w, 2, source(2)).wait_recv()
+                hand(l, core, w, 2).start()
+
+        if square:
+            by_core(work)
+
+    def wait_weights(l, k):
+        def work(core):
+            for w in KINDS[k]:
+                for slot in slots:
+                    hand(l, 1 - core, w, slot).wait_recv()
 
         by_core(work)
-        for w in range(4):
+        for w in KINDS[k]:
             own(l, w).wait()
 
-    def end_weights(l):
+    def end_weights():
         def work(core):
-            for i, d in pieces(core):
-                push(l, core, i, d).wait_send()
-                hand(l, core, i, d).wait_send()
+            for l in range(2):
+                for w in range(4):
+                    for slot in direct:
+                        push(l, core, w, slot).wait_send()
+                    if square:
+                        relay(l, core, w).wait_send()
+                    for slot in slots:
+                        hand(l, core, w, slot).wait_send()
 
         by_core(work)
 
     def vector_copy(d):
         return remote(
-            vec_i, vec_got.at[place.row], vec_sem.at[0, d - 1], vec_sem.at[1, d - 1], place.in_row(d)
+            vec_mine,
+            vec_got.at[place.row],
+            vec_sem.at[0, d - 1],
+            vec_sem.at[1, d - 1],
+            place.in_row(d),
         )
 
-    def edge_copy(which, d):
+    def edge_copy(which):
         return remote(
             edge_out.at[which],
             edge_in.at[which],
             edge_sem.at[0, which],
             edge_sem.at[1, which],
-            place.in_row(d),
+            place.in_row(1 if which == 2 else n_row - 1),
         )
 
-    def pack_edge(which, source, first_window, first_sub):
+    def pack_edge(which, values, first_window, first_sub):
         for col in range(WIN_COLS):
             at = CELL * (first_window + col) + BLOCK * first_sub
-            edge_out[which, 2 * BLOCK * col : 2 * BLOCK * (col + 1), :] = source[
+            edge_out[which, 2 * BLOCK * col : 2 * BLOCK * (col + 1), :] = values[
                 at : at + 2 * BLOCK, :
             ].astype(bf16)
 
-    def pick_rows(source, target):
+    def pick_rows(values, out):
         for c in range(chunks):
             rows = slice(CHUNK * c, CHUNK * (c + 1))
             spots = lax.broadcasted_iota(jnp.int32, (CHUNK, tokens), 1)
             pick = jnp.where(spots == place_col[rows, :], 1.0, 0.0).astype(bf16)
-            target[rows, :] = dot_nn(pick, source[...]).astype(target.dtype)
+            out[rows, :] = dot_nn(pick, values[...]).astype(out.dtype)
 
     @pl.when(step == 0)
     def _():
         for l in range(2):
             for w in range(4):
                 own(l, w).start()
-        mine = pltpu.make_async_copy(vec_i, vec_got.at[place.row], out_sem.at[4])
-        mine.start()
         if swap:
             swap_own(place, x_in, x_got, x_sem).start()
             swap_own(place, c_in, c_got, c_sem).start()
@@ -508,10 +567,32 @@
             swap_start(place, x_in, x_got, x_sem)
         else:
             meet(place.partners(far=False))
+        start_weights(0, 0)
+        vec_wide[...] = jnp.zeros_like(vec_wide)
+        for l in range(2):
+            parts = (
+                qv_bias[l],
+                proj_bias[l : l + 1],
+                fc2_bias[l : l + 1],
+                gain_ref[l],
+                shift_ref[l],
+            )
+            vec_wide[16 * l : 16 * l + 8, 0:size] = jnp.concatenate(
+                [part.astype(f32) for part in parts], axis=0
+            )
+            vec_wide[16 * l + 8 : 16 * l + 9, 0 : 4 * size] = fc1_bias[l : l + 1].astype(f32)
+        vec_mine[...] = vec_wide[...].astype(bf16)
         for d in range(1, n_row):
             vector_copy(d).start()
-        start_weights(0)
-        bias_rows(table_ref, lanes_ref, order_ref, bias_s, wide_s)
+        mine = pltpu.make_async_copy(vec_mine, vec_got.at[place.row], out_sem.at[4])
+        mine.start()
+        eye = lax.broadcasted_iota(jnp.int32, (TABLE, TABLE_PAD), 0) == lax.broadcasted_iota(
+            jnp.int32, (TABLE, TABLE_PAD), 1
+        )
+        eye = jnp.where(eye, 1.0, 0.0).astype(bf16)
+        for l in range(2):
+            table_s[l] = sum(dot_tn(part, eye) for part in reversed(split(table_ref[l])))
+        bias_rows(table_s, lanes_ref, order_ref, bias_s, wide_s)
         mine.wait()
         for d in range(1, n_row):
             vector_copy(d).wait()
@@ -525,100 +606,135 @@
             fc1_b[l, 0:1, :] = jnp.concatenate(
                 [share[8:9, 0 : 4 * size] for share in shares], axis=1
             )
+        pass_weights(0, 0)
+        start_weights(0, 1)
         if swap:
             swap_wait(place, x_in, x_got, x_sem)
             swap_own(place, x_in, x_got, x_sem).wait()
         pick_rows(x_got, x_s)
-        pass_weights(0)
-        wait_weights(0)
+        pass_relayed(0, 0)
+        wait_weights(0, 0)
+        start_weights(1, 0)
 
     @pl.when(step == 1)
     def _():
-        start_weights(1)
+        pass_weights(0, 1)
+
+    @pl.when(step == chunks - 1)
+    def _():
+        pass_relayed(0, 1)
+        start_weights(1, 1)
+
+    @pl.when(step == chunks)
+    def _():
+        wait_weights(0, 1)
+        pass_weights(1, 0)
         if swap:
             swap_start(place, c_in, c_got, c_sem)
 
-    @pl.when(step == chunks - 1)
-    def _():
-        pass_weights(1)
-
-    @pl.when(step == chunks)
-    def _():
-        wait_weights(1)
+    @pl.when(step == chunks + 2)
+    def _():
+        pass_relayed(1, 0)
+
+    @pl.when(step == 2 * chunks - 1)
+    def _():
+        pass_weights(1, 1)
+
+    @pl.when(step == 2 * chunks)
+    def _():
+        wait_weights(1, 0)
+        assemble_ahead(y_s, edge_in.at[0], x_s, range(window_rows - 1))
+
+    @pl.when(step == 2 * chunks + chunks // 2)
+    def _():
+        pass_relayed(1, 1)
+        edge_copy(0).wait_recv()
+        assemble_ahead(y_s, edge_in.at[0], x_s, range(window_rows - 1, window_rows))
+
+    @pl.when(step == 3 * chunks)
+    def _():
+        wait_weights(1, 1)
         for w in range(4):
             pltpu.make_async_copy(kept[w], outs[w], out_sem.at[w]).start()
-        edge_copy(0, n_row - 1).wait_recv()
-        assemble_ahead(y_s, edge_in.at[0], x_s)
-
-    @pl.when(step == chunks + 2)
-    def _():
         if swap:
             swap_wait(place, c_in, c_got, c_sem)
             swap_own(place, c_in, c_got, c_sem).wait()
         pick_rows(c_got, c_s)
-        pack_edge(2, c_s, 0, 0)
-        edge_copy(2, n_row - 1).start()
+        pack_edge(1, c_s, 0, 0)
+        edge_copy(1).start()
 
     here = pl.ds(pl.multiple_of(chunk * CHUNK, CHUNK), CHUNK)
-    x = x_s[here, :]
-    x_out[0] = x
-    normal, _ = norm_parts(x)
-    hidden = (normal * vec_out[layer, 4:5, :] + vec_out[layer, 6:7, :]).astype(bf16)
-    qkv_out[0] = (dot_nn(hidden, qkv_s[layer]) + qkv_b[layer]).astype(bf16)
-    wide = (CELL, GROUP * CELL)
-    apart = lax.broadcasted_iota(jnp.int32, wide, 0) ^ lax.broadcasted_iota(jnp.int32, wide, 1)
-    for k in range(CHUNK_WINS):
-        rows = slice(CELL * k, CELL * (k + 1))
-        keep = (apart & cuts_ref[(layer * chunks + chunk) * CHUNK_WINS + k]) == 0
-        mixed = []
-        for g in range(2):
-            q = qkv_out[0, rows, 128 * g : 128 * g + 256]
-            key = qkv_out[0, rows, D + 128 * g : D + 128 * g + 256]
-            val = qkv_out[0, rows, 2 * D + 128 * g : 2 * D + 128 * g + 256]
-            q_wide = jnp.concatenate([q] * GROUP, axis=0) * wide_heads_ref[g]
-            lanes = slice(GROUP * CELL * g, GROUP * CELL * (g + 1))
-            s = dot_nt(key, q_wide) * SCALE + bias_s[layer, :, lanes]
-            s = jnp.where(keep, s, MASKED)
-            e = jnp.exp(s - jnp.max(s, axis=0, keepdims=True))
-            prob = (e * (1.0 / jnp.sum(e, axis=0, keepdims=True))).astype(bf16)
-            prob_out[0, rows, lanes] = prob
-            mixed.append(gather_heads(dot_tn(prob, val), heads_ref, g))
-        att_out[0, rows, :] = join_groups(*mixed).astype(bf16)
-    mid = x + (dot_nn(att_out[0], proj_s[layer]) + vec_out[layer, 2:3, :])
-    mid_out[0] = mid
-    normal, _ = norm_parts(mid)
-    hidden = (normal * vec_out[layer, 5:6, :] + vec_out[layer, 7:8, :]).astype(bf16)
-    u = dot_nn(hidden, fc1_s[layer]) + fc1_b[layer]
-    cdf = 0.5 * (1.0 + lax.erf(u * ROOT_HALF))
-    act_out[0] = (u * cdf).astype(bf16)
-    slope_out[0] = (cdf + u * (jnp.exp(-0.5 * u * u) * INV_ROOT_TAU)).astype(bf16)
-    y_s[here, :] = mid + (dot_nn(act_out[0], fc2_s[layer]) + vec_out[layer, 3:4, :])
-
-    @pl.when(step == chunks // 2 - 1)
+
+    @pl.when(kind == 0)
+    def _():
+        x = x_s[here, :]
+        x_out[0] = x
+        normal, _ = norm_parts(x)
+        hidden = (normal * vec_out[layer, 4:5, :] + vec_out[layer, 6:7, :]).astype(bf16)
+        qkv_out[0] = (dot_nn(hidden, qkv_s[layer]) + qkv_b[layer]).astype(bf16)
+        wide = (CELL, GROUP * CELL)
+        apart = lax.broadcasted_iota(jnp.int32, wide, 0) ^ lax.broadcasted_iota(jnp.int32, wide, 1)
+        for k in range(CHUNK_WINS):
+            rows = slice(CELL * k, CELL * (k + 1))
+            window = chunk * CHUNK_WINS + k
+            middle = (place.row * window_rows + window // WIN_COLS + 1) * WIN
+            row_cut = (middle == split_ref[0]) | (middle == n_row * window_rows * WIN)
+            col_cut = window % WIN_COLS == WIN_COLS - 1
+            cut = layer * (jnp.where(row_cut, 32, 0) + jnp.where(col_cut, 16, 0))
+            keep = (apart & cut) == 0
+            mixed = []
+            for g in range(2):
+                q = qkv_out[0, rows, 128 * g : 128 * g + 256]
+                key = qkv_out[0, rows, D + 128 * g : D + 128 * g + 256]
+                val = qkv_out[0, rows, 2 * D + 128 * g : 2 * D + 128 * g + 256]
+                q_wide = jnp.concatenate([q] * GROUP, axis=0) * wide_heads_ref[g]
+                lanes = slice(GROUP * CELL * g, GROUP * CELL * (g + 1))
+                scores = dot_nt(key, q_wide) * SCALE + bias_s[layer, :, lanes]
+                scores = jnp.where(keep, scores, MASKED)
+                e = jnp.exp(scores - jnp.max(scores, axis=0, keepdims=True))
+                prob = (e * (1.0 / jnp.sum(e, axis=0, keepdims=True))).astype(bf16)
+                prob_out[0, rows, lanes] = prob
+                mixed.append(gather_heads(dot_tn(prob, val), heads_ref, g))
+            att_out[0, rows, :] = join_groups(*mixed).astype(bf16)
+        mid = x + (dot_nn(att_out[0], proj_s[layer]) + vec_out[layer, 2:3, :])
+        x_s[here, :] = mid
+        mid_out[0] = mid
+
+    @pl.when(kind == 1)
+    def _():
+        mid = x_s[here, :]
+        normal, _ = norm_parts(mid)
+        hidden = (normal * vec_out[layer, 5:6, :] + vec_out[layer, 7:8, :]).astype(bf16)
+        u = dot_nn(hidden, fc1_s[layer]) + fc1_b[layer]
+        cdf = 0.5 * (1.0 + lax.erf(u * ROOT_HALF))
+        act_out[0] = (u * cdf).astype(bf16)
+        slope_out[0] = (cdf + u * (jnp.exp(-0.5 * u * u) * INV_ROOT_TAU)).astype(bf16)
+        y_s[here, :] = mid + (dot_nn(act_out[0], fc2_s[layer]) + vec_out[layer, 3:4, :])
+
+    @pl.when(step == chunks + chunks // 2 - 1)
     def _():
         pack_edge(0, y_s, 0, 0)
-        edge_copy(0, n_row - 1).start()
-
-    @pl.when(step == chunks + chunks // 2 - 1)
-    def _():
-        pack_edge(1, y_s, last_row, 2)
-        edge_copy(1, 1).start()
-
-    @pl.when(step == 2 * chunks - 1)
-    def _():
-        edge_copy(2, n_row - 1).wait_recv()
-        assemble_ahead(c_s, edge_in.at[2], up_out)
-        edge_copy(1, 1).wait_recv()
-        assemble_back(y_s, edge_in.at[1], c_s)
+        edge_copy(0).start()
+
+    @pl.when(step == 3 * chunks + chunks // 2 - 1)
+    def _():
+        pack_edge(2, y_s, last_row, 2)
+        edge_copy(2).start()
+
+    @pl.when(step == 4 * chunks - 1)
+    def _():
+        edge_copy(2).wait_recv()
+        assemble_back(y_s, edge_in.at[2], order_s)
         for c in range(chunks):
             rows = slice(CHUNK * c, CHUNK * (c + 1))
             spots = lax.broadcasted_iota(jnp.int32, (CHUNK, tokens), 0) + CHUNK * c
             pick = jnp.where(spots == place_row[...], 1.0, 0.0).astype(bf16)
-            rows_out[rows, :] = dot_nn(pick, c_s[...]).astype(bf16)
-        for l in range(2):
-            end_weights(l)
+            y_out[rows, :] = dot_nn(pick, order_s[...]).astype(bf16)
+        edge_copy(1).wait_recv()
+        assemble_ahead(c_s, edge_in.at[1], up_out, range(window_rows))
+        end_weights()
         for which in range(3):
-            edge_copy(which, 1 if which == 1 else n_row - 1).wait_send()
+            edge_copy(which).wait_send()
         for w in range(4):
             pltpu.make_async_copy(kept[w], outs[w], out_sem.at[w]).wait()
         if swap:
@@ -640,19 +756,20 @@
     return jnp.concatenate([low[:, :128], low[:, 128:] + high[:, :128], high[:, 128:]], axis=1)
 
 
-def forward_layers(cuts, placing, x_in, c_in, shards, vectors, rel_table):
+def forward_layers(split_row, placing, x_in, c_in, shards, vectors, rel_table):
     n_row, n_far = lax.axis_size("row"), lax.axis_size("clip") // 2
+    n = 2 * n_row * n_far
     tokens = x_in.shape[0]
     chunks = tokens // CHUNK
-    swap = can_swap(tokens, n_row * n_far * 2)
+    swap = can_swap(tokens, n)
     heads, wide = head_masks()
     lanes, order, _ = table_constants()
-    table = jnp.pad(rel_table.transpose(0, 2, 1), ((0, 0), (0, 0), (0, TABLE_PAD - TABLE)))
     ff = shards[2].shape[2]
     anywhere = pl.BlockSpec(memory_space=pl.ANY)
     patches = anywhere if swap else whole((tokens, D))
-    constants = (
-        table,
+    small = (
+        *vectors,
+        rel_table,
         jnp.asarray(lanes.reshape(2 * TABLE_PAD, 128), dtype=bf16),
         jnp.asarray(order, dtype=bf16),
         jnp.asarray(heads),
@@ -660,16 +777,28 @@
     )
     full = [(2, shard.shape[1] * n_row, shard.shape[2]) for shard in shards]
 
-    def block(i):
-        layer = i // chunks
-        return layer, (i + layer * (chunks // 2)) % chunks, 0
-
-    saved = [(D, f32), (3 * D, bf16), (HEADS * CELL, bf16), (D, bf16), (D, f32), (ff, bf16), (ff, bf16)]
+    def attention_block(i):
+        kind = i // chunks % 2
+        return i // (2 * chunks), (1 - kind) * (i % chunks) + kind * (chunks - 1), 0
+
+    def forward_block(i):
+        layer, kind = i // (2 * chunks), i // chunks % 2
+        half = layer * (chunks // 2)
+        return layer, kind * ((i + half) % chunks) + (1 - kind) * half, 0
+
+    saved = [
+        (D, f32, attention_block),
+        (3 * D, bf16, attention_block),
+        (HEADS * CELL, bf16, attention_block),
+        (D, bf16, attention_block),
+        (D, f32, attention_block),
+        (ff, bf16, forward_block),
+        (ff, bf16, forward_block),
+    ]
     dma = pltpu.SemaphoreType.DMA
-    n = n_row * n_far * 2
     results = pl.pallas_call(
         functools.partial(forward_kernel, n_row, n_far, swap),
-        grid=(2 * chunks,),
+        grid=(4 * chunks,),
         in_specs=[
             pl.BlockSpec(memory_space=pltpu.SMEM),
             whole((tokens, 1)),
@@ -677,13 +806,13 @@
             patches,
             patches,
         ]
-        + [anywhere] * 5
-        + [whole(constant.shape) for constant in constants],
-        out_specs=[pl.BlockSpec((1, CHUNK, width), block) for width, _ in saved]
+        + [anywhere] * 4
+        + [whole(value.shape) for value in small],
+        out_specs=[pl.BlockSpec((1, CHUNK, width), block) for width, _, block in saved]
         + [whole((tokens, D))] * 2
         + [anywhere] * 4
         + [whole((2, 8, D))],
-        out_shape=[jax.ShapeDtypeStruct((2, tokens, width), kind) for width, kind in saved]
+        out_shape=[jax.ShapeDtypeStruct((2, tokens, width), kind) for width, kind, _ in saved]
         + [jax.ShapeDtypeStruct((tokens, D), bf16)] * 2
         + [jax.ShapeDtypeStruct(shape, bf16) for shape in full]
         + [jax.ShapeDtypeStruct((2, 8, D), f32)],
@@ -691,21 +820,25 @@
             pltpu.VMEM((tokens if swap else 16, D), bf16),
             pltpu.VMEM((tokens if swap else 16, D), bf16),
             *[pltpu.VMEM(shape, bf16) for shape in full],
-            pltpu.VMEM((n_row, *vectors.shape), bf16),
+            pltpu.VMEM((32, D), f32),
+            pltpu.VMEM((32, D), bf16),
+            pltpu.VMEM((n_row, 32, D), bf16),
             pltpu.VMEM((2, 1, 3 * D), f32),
             pltpu.VMEM((2, 1, ff), f32),
+            pltpu.VMEM((2, HEADS, TABLE_PAD), f32),
             pltpu.VMEM((2, CELL, HEADS * CELL), f32),
             pltpu.VMEM((HEADS // 2 * CELL, 2 * TABLE_PAD), f32),
             pltpu.VMEM((tokens, D), f32),
             pltpu.VMEM((tokens, D), f32),
+            pltpu.VMEM((tokens, D), bf16),
             pltpu.VMEM((tokens, D), bf16),
             pltpu.VMEM((3, WIN_COLS * 2 * BLOCK, D), bf16),
             pltpu.VMEM((3, WIN_COLS * 2 * BLOCK, D), bf16),
             dma((2, n if swap else 1)),
             dma((2, n if swap else 1)),
             dma((2, 4)),
-            dma((2, 2, 3, n_row - 1)),
-            dma((2, 2, 3, n_row - 1)),
+            dma((2, 2, 4, n_row - 1)),
+            dma((2, 2, 4, n_row - 1)),
             dma((2, n_row - 1)),
             dma((2, 3)),
             dma((5,)),
@@ -714,15 +847,25 @@
             collective_id=0, has_side_effects=True, vmem_limit_bytes=VMEM_LIMIT
         ),
         name="forward_layers",
-    )(cuts, placing.reshape(tokens, 1), placing.reshape(1, tokens), x_in, c_in, *shards, vectors, *constants)
+    )(
+        split_row,
+        placing.reshape(tokens, 1),
+        placing.reshape(1, tokens),
+        x_in,
+        c_in,
+        *shards,
+        *small,
+    )
     return results[:7], results[7], results[8], results[9:13], results[13]
 
 
-BATCHES = ((1, 0), (1, 1), (0, 0), (0, 1))
+BATCHES = ((1, 0), (1, 1), (1, 2), (0, 0), (0, 1), (0, 2))
 
 
 def batch_rows(n_row, kind):
-    return 4 * row_share(n_row) if kind == 0 else 2 * row_share(n_row) + 16
+    size = row_share(n_row)
+    low = shard_half(size, 0)[1]
+    return (2 * size, 2 * size + low, size + low + 16)[kind]
 
 
 def piece_rows(n_row, n_far, kind):
@@ -754,8 +897,9 @@
     back_ref,
     rows_out,
     grad_out,
-    final_m_out,
-    final_a_out,
+    final_0,
+    final_1,
+    final_2,
     vec_g,
     fc1_bg,
     table_g,
@@ -769,28 +913,10 @@
     grad_rows,
     edge_out,
     edge_in,
-    pack_m,
-    pack_a,
-    got_am,
-    got_aa,
-    got_bm,
-    got_ba,
-    out_cm,
-    out_ca,
-    got_cm,
-    got_ca,
-    final_m,
-    final_a,
-    rows_sem,
-    grad_sem,
-    edge_sem,
-    a_sem,
-    b_sem,
-    c_sem,
-    d_sem,
-    e_sem,
-    done_sem,
+    *refs,
 ):
+    packs, got_as, got_bs, out_cs, got_cs, finals = (refs[3 * i : 3 * i + 3] for i in range(6))
+    rows_sem, grad_sem, edge_sem, a_sem, b_sem, c_sem, d_sem, e_sem, done_sem = refs[18:]
     step = pl.program_id(0)
     tokens = g_s.shape[1]
     chunks = tokens // CHUNK
@@ -800,15 +926,26 @@
     place = Place(n_row, n_far)
     core, row, far = place.core, place.row, place.far
     size = row_share(n_row)
+    low = shard_half(size, 0)[1]
     last_row = (tokens // CELL // WIN_COLS - 1) * WIN_COLS
-    packs, got_as, got_bs = (pack_m, pack_a), (got_am, got_aa), (got_bm, got_ba)
-    out_cs, got_cs, finals = (out_cm, out_ca), (got_cm, got_ca), (final_m, final_a)
     here = pl.ds(pl.multiple_of(chunk * CHUNK, CHUNK), CHUNK)
 
     def edge_copy():
-        return remote(
-            edge_out, edge_in, edge_sem.at[0], edge_sem.at[1], place.in_row(1)
-        )
+        return remote(edge_out, edge_in, edge_sem.at[0], edge_sem.at[1], place.in_row(1))
+
+    def start_rows(source, target, sem):
+        if swap:
+            swap_own(place, source, target, sem).start()
+            swap_start(place, source, target, sem)
+        else:
+            pltpu.make_async_copy(source, target, sem.at[0, 0]).start()
+
+    def unpick_rows(values, out):
+        for c in range(chunks):
+            rows = slice(CHUNK * c, CHUNK * (c + 1))
+            spots = lax.broadcasted_iota(jnp.int32, (CHUNK, tokens), 0) + CHUNK * c
+            pick = jnp.where(spots == place_row[...], 1.0, 0.0).astype(bf16)
+            out[rows, :] = dot_nn(pick, values).astype(bf16)
 
     def part(ref, b, at):
         rows = got_cs[BATCHES[b][1]].shape[2]
@@ -842,9 +979,7 @@
 
     def copy_d(b, d, owner):
         spot = part(finals[BATCHES[b][1]].at[core], b, owner)
-        return remote(
-            spot, spot, d_sem.at[0, b, d - 1], d_sem.at[1, b, d - 1], place.along(d)
-        )
+        return remote(spot, spot, d_sem.at[0, b, d - 1], d_sem.at[1, b, d - 1], place.along(d))
 
     def copy_e(b, d, half):
         spot = part(finals[BATCHES[b][1]].at[half], b, place.far_at((n_far - d) % n_far))
@@ -896,66 +1031,80 @@
             copy_e(b, d, core).wait_send()
             copy_e(b, d, 1 - core).wait_recv()
 
+    stages = [sum_cores, sum_row, sum_far, pass_on]
+
+    visits = {
+        2: (0,),
+        chunks + 1: (0, 1),
+        2 * chunks - 1: (0,),
+        2 * chunks: (1,),
+        2 * chunks + 1: (0, 2, 3),
+        2 * chunks + 2: (1,),
+        3 * chunks: (2,),
+        3 * chunks + 1: (1, 4),
+        3 * chunks + 2: (2, 3),
+    }
+    reached = [0] * len(BATCHES)
+
+    def advance(b):
+        for stage in stages[reached[b] : reached[b] + 1]:
+            stage(b)
+        reached[b] += 1
+
     @pl.when(step == 0)
     def _():
         if swap:
-            swap_own(place, rows_in, rows_out, rows_sem).start()
             meet_all(place)
-            swap_start(place, rows_in, rows_out, rows_sem)
         else:
-            pltpu.make_async_copy(rows_in, rows_out, rows_sem.at[0, 0]).start()
             meet(place.partners())
+        start_rows(rows_in, rows_out, rows_sem)
         g_s[1] = up_ref[...].astype(f32)
-        for k in range(2):
+        for k in range(3):
             valid, padded = batch_rows(n_row, k), out_cs[k].shape[1]
             if padded > valid:
                 out_cs[k][:, valid:, :] = jnp.zeros((2, padded - valid, D), bf16)
-
-    @pl.when(step == chunks + 1)
-    def _():
-        sum_cores(0)
+        if 2 * low > size:
+            spare = (2, n_row, 2 * low - size, D)
+            packs[1][:, 1, :, 3 * size - low :, :] = jnp.zeros(spare, bf16)
+            packs[2][:, 1, :, 2 * size - low : size + low, :] = jnp.zeros(spare, bf16)
 
     @pl.when(step == 2 * chunks)
     def _():
         edge_copy().wait_recv()
         assemble_back(g_s.at[1], edge_in, g_s.at[0])
-        sum_row(0)
-
-    @pl.when(step == 2 * chunks + 1)
-    def _():
-        sum_cores(1)
-
-    @pl.when(step == 2 * chunks + 2)
-    def _():
-        sum_far(0)
-
-    @pl.when(step == 3 * chunks - 1)
-    def _():
-        sum_row(1)
-        pass_on(0)
-
-    @pl.when(step == 3 * chunks)
-    def _():
-        sum_far(1)
-
-    @pl.when(step == 3 * chunks + 1)
-    def _():
-        sum_cores(2)
-        pass_on(1)
+
+    for at, due in visits.items():
+
+        @pl.when(step == at)
+        def _():
+            for b in due:
+                advance(b)
 
     @pl.when(step % (2 * chunks) == 0)
     def _():
         vec_g[...] = jnp.zeros_like(vec_g)
         fc1_bg[...] = jnp.zeros_like(fc1_bg)
         table_g[...] = jnp.zeros_like(table_g)
+        gz_s[...] = g_s[layer].astype(bf16)
+        vec_g[3:4, :] = column_sum(gz_s[...].astype(f32))
+        count = D // (4 * size)
+        for j in range(4):
+            value = dot_tn(act_ref[0, :, D * j : D * (j + 1)], gz_s[...]).astype(bf16)
+            for t in range(count):
+                for half in range(2):
+                    at = (2 * t + half) * 2 * size
+                    packs[0][layer, half, j * count + t] = value[at : at + 2 * size, :]
+
+    for b in (0, 3):
+
+        @pl.when(step == 2 * chunks * (b // 3))
+        def _():
+            copy_a(b).start()
 
     @pl.when(kind == 0)
     def _():
         upstream = g_s[layer, here, :]
-        low = upstream.astype(bf16)
-        gz_s[here, :] = low
-        vec_g[3:4, :] += column_sum(low.astype(f32))
-        du = (dot_nt(low, fc2_w[0]) * slope_ref[0].astype(f32)).astype(bf16)
+        du = (dot_nt(gz_s[here, :], fc2_w[0]) * slope_ref[0].astype(f32)).astype(bf16)
         du_s[here, :] = du
         fc1_bg[...] += column_sum(du.astype(f32))
         dn = dot_nt(du, fc1_w[0])
@@ -966,31 +1115,30 @@
         vec_g[7:8, :] += column_sum(dn)
         mid_grad = upstream + norm_back(dn, normal, inverse, gain)
         g_s[layer, here, :] = mid_grad
-        low = mid_grad.astype(bf16)
-        ga_s[here, :] = low
-        vec_g[2:3, :] += column_sum(low.astype(f32))
+        branch = mid_grad.astype(bf16)
+        ga_s[here, :] = branch
+        vec_g[2:3, :] += column_sum(branch.astype(f32))
+
+    def put(k, half, at, value, first, count):
+        for r in range(n_row):
+            packs[k][layer, half, r, at : at + count, :] = value[
+                size * r + first : size * r + first + count, :
+            ]
 
     @pl.when(step % (2 * chunks) == chunks - 1)
     def _():
         for j in range(4):
-            lanes = slice(D * j, D * (j + 1))
-            value = dot_tn(h2_s[...], du_s[:, lanes]).astype(bf16)
-            for r in range(n_row):
-                pack_m[layer, 0, r, size * j : size * (j + 1), :] = value[
-                    size * r : size * (r + 1), :
-                ]
-            value = dot_tn(act_ref[0, :, lanes], gz_s[...]).astype(bf16)
-            count = D // (4 * size)
-            for t in range(count):
-                pack_m[layer, 1, j * count + t] = value[4 * size * t : 4 * size * (t + 1), :]
-
-    @pl.when(step == chunks - 1)
-    def _():
-        copy_a(0).start()
-
-    @pl.when(step == 3 * chunks - 1)
-    def _():
-        copy_a(2).start()
+            value = dot_tn(h2_s[...], du_s[:, D * j : D * (j + 1)]).astype(bf16)
+            put(1, j // 2, size * (j % 2), value, 0, size)
+        value = dot_tn(att_ref[0], ga_s[...]).astype(bf16)
+        put(1, 0, 2 * size, value, 0, low)
+        put(1, 1, 2 * size, value, low, size - low)
+
+    for b in (1, 4):
+
+        @pl.when(step == 2 * chunks * (b // 3) + chunks - 1)
+        def _():
+            copy_a(b).start()
 
     @pl.when(kind == 1)
     def _():
@@ -1041,28 +1189,16 @@
 
     @pl.when(step == 4 * chunks - 1)
     def _():
-        source = g_s[0].astype(bf16)
-        for c in range(chunks):
-            rows = slice(CHUNK * c, CHUNK * (c + 1))
-            spots = lax.broadcasted_iota(jnp.int32, (CHUNK, tokens), 0) + CHUNK * c
-            pick = jnp.where(spots == place_row[...], 1.0, 0.0).astype(bf16)
-            grad_rows[rows, :] = dot_nn(pick, source).astype(bf16)
-        if swap:
-            swap_own(place, grad_rows, grad_out, grad_sem).start()
-            swap_start(place, grad_rows, grad_out, grad_sem)
-        else:
-            pltpu.make_async_copy(grad_rows, grad_out, grad_sem.at[0, 0]).start()
+        for b in (4, 3, 2):
+            advance(b)
 
     @pl.when(step % (2 * chunks) == 2 * chunks - 1)
     def _():
-        def put(half, at, value):
-            for r in range(n_row):
-                pack_a[layer, half, r, at : at + size, :] = value[size * r : size * (r + 1), :]
-
-        for j in range(3):
-            value = dot_tn(h1_s[...], dt_s[:, D * j : D * (j + 1)]).astype(bf16)
-            put(j // 2, size * (j % 2), value)
-        put(1, size, dot_tn(att_ref[0], ga_s[...]).astype(bf16))
+        values = [dot_tn(h1_s[...], dt_s[:, D * j : D * (j + 1)]).astype(bf16) for j in range(3)]
+        put(2, 0, 0, values[0], 0, size)
+        put(2, 0, size, values[1], 0, low)
+        put(2, 1, 0, values[2], 0, size)
+        put(2, 1, size, values[1], low, size - low)
         table = table_rows(table_g[...], lanes_ref, back_ref)
         table = jnp.concatenate([table, jnp.zeros((HEADS, D - TABLE_PAD), f32)], axis=1)
         vectors = jnp.concatenate(
@@ -1072,29 +1208,27 @@
             axis=0,
         )
         for r in range(n_row):
-            pack_a[layer, 0, r, 2 * size :, :] = vectors.astype(bf16)
-            pack_a[layer, 1, r, 2 * size :, :] = table.astype(bf16)
+            packs[2][layer, 0, r, size + low :, :] = vectors.astype(bf16)
+            packs[2][layer, 1, r, size + low :, :] = table.astype(bf16)
 
     @pl.when(step == 2 * chunks - 1)
     def _():
-        copy_a(1).start()
+        copy_a(2).start()
 
     @pl.when(step == 4 * chunks - 1)
     def _():
-        copy_a(3).start()
-        sum_row(2)
-        sum_cores(3)
-        sum_far(2)
-        sum_row(3)
-        pass_on(2)
-        sum_far(3)
-        pass_on(3)
-        for b in range(4):
+        copy_a(5).start()
+        unpick_rows(g_s[0].astype(bf16), grad_rows)
+        start_rows(grad_rows, grad_out, grad_sem)
+        while min(reached) < len(stages):
+            for b in (5, 4, 3, 2, 1, 0):
+                advance(b)
+        for b in range(len(BATCHES)):
             finish(b)
         edge_copy().wait_send()
         copies = [
-            pltpu.make_async_copy(final_m, final_m_out, done_sem.at[0]),
-            pltpu.make_async_copy(final_a, final_a_out, done_sem.at[1]),
+            pltpu.make_async_copy(finals[k], out, done_sem.at[k])
+            for k, out in enumerate((final_0, final_1, final_2))
         ]
         for copy in copies:
             copy.start()
@@ -1112,7 +1246,7 @@
                 pltpu.make_async_copy(source, target, sem.at[0, 0]).wait()
 
 
-def backward_layers(placing, upstream, rows, saved, full, vec):
+def backward_layers(placing, upstream, y, saved, full, vec):
     n_row, n_far = lax.axis_size("row"), lax.axis_size("clip") // 2
     n = 2 * n_row * n_far
     tokens = upstream.shape[0]
@@ -1152,13 +1286,13 @@
         jnp.asarray(lanes.reshape(2 * TABLE_PAD, 128), dtype=bf16),
         jnp.asarray(back, dtype=bf16),
     )
-    valid = [batch_rows(n_row, k) for k in range(2)]
-    piece = [piece_rows(n_row, n_far, k) for k in range(2)]
-    final = [(2, 2, n_far * piece[k], D) for k in range(2)]
+    valid = [batch_rows(n_row, k) for k in range(3)]
+    piece = [piece_rows(n_row, n_far, k) for k in range(3)]
+    final = [(2, 2, n_far * piece[k], D) for k in range(3)]
     dma = pltpu.SemaphoreType.DMA
 
-    def pair(shape_of):
-        return [pltpu.VMEM(shape_of(k), bf16) for k in range(2)]
+    def each(shape_of):
+        return [pltpu.VMEM(shape_of(k), bf16) for k in range(3)]
 
     return pl.pallas_call(
         functools.partial(backward_kernel, n_row, n_far, swap),
@@ -1166,7 +1300,7 @@
         in_specs=[
             whole((1, tokens)),
             whole((tokens, D)),
-            anywhere,
+            whole((tokens, D)),
             chunked(x, attention_block),
             chunked(qkv, attention_block),
             chunked(prob, attention_block),
@@ -1177,7 +1311,7 @@
         ]
         + [layered(weight) for weight in full]
         + [whole(constant.shape) for constant in constants],
-        out_specs=[anywhere] * 4,
+        out_specs=[anywhere] * 5,
         out_shape=[jax.ShapeDtypeStruct((tokens, D), bf16)] * 2
         + [jax.ShapeDtypeStruct(shape, bf16) for shape in final],
         scratch_shapes=[
@@ -1190,35 +1324,34 @@
             pltpu.VMEM((tokens, D), bf16),
             pltpu.VMEM((tokens, D), bf16),
             pltpu.VMEM((tokens, ff), bf16),
-            pltpu.VMEM((tokens, D), bf16),
-            pltpu.VMEM((tokens, D), bf16),
+            *[pltpu.VMEM((tokens, D), bf16)] * 2,
             pltpu.VMEM((WIN_COLS * 2 * BLOCK, D), bf16),
             pltpu.VMEM((WIN_COLS * 2 * BLOCK, D), bf16),
-            *pair(lambda k: (2, 2, n_row, valid[k], D)),
-            *pair(lambda k: (2, n_row, valid[k], D)),
-            *pair(lambda k: (2, n_row - 1, valid[k], D)),
-            *pair(lambda k: (2, n_far * piece[k], D)),
-            *pair(lambda k: (2, n_far - 1, piece[k], D)),
-            *pair(lambda k: final[k]),
+            *each(lambda k: (2, 2, n_row, valid[k], D)),
+            *each(lambda k: (2, n_row, valid[k], D)),
+            *each(lambda k: (2, n_row - 1, valid[k], D)),
+            *each(lambda k: (2, n_far * piece[k], D)),
+            *each(lambda k: (2, n_far - 1, piece[k], D)),
+            *each(lambda k: final[k]),
             dma((2, n if swap else 1)),
             dma((2, n if swap else 1)),
             dma((2,)),
-            dma((2, 4)),
-            dma((2, 4, n_row - 1)),
-            dma((2, 4, n_far - 1)),
-            dma((2, 4, n_far - 1)),
-            dma((2, 4, n_far)),
-            dma((2,)),
+            dma((2, len(BATCHES))),
+            dma((2, len(BATCHES), n_row - 1)),
+            dma((2, len(BATCHES), n_far - 1)),
+            dma((2, len(BATCHES), n_far - 1)),
+            dma((2, len(BATCHES), n_far)),
+            dma((3,)),
         ],
         compiler_params=pltpu.CompilerParams(
             collective_id=1, has_side_effects=True, vmem_limit_bytes=VMEM_LIMIT
         ),
         name="backward_layers",
-    )(placing.reshape(1, tokens), upstream, rows, x, qkv, prob, att, mid, act, slope, *full, *constants)
+    )(placing.reshape(1, tokens), upstream, y, x, qkv, prob, att, mid, act, slope, *full, *constants)
 
 
 def unpack_kernel(
-    n_row, m_ref, a_ref, qkv_o, qvb_o, proj_o, projb_o, fc1_o, fc1b_o, fc2_o, fc2b_o, gain_o, shift_o, table_o
+    n_row, fc2_ref, fc1_ref, qkv_ref, qkv_o, qvb_o, proj_o, projb_o, fc1_o, fc1b_o, fc2_o, fc2b_o, gain_o, shift_o, table_o
 ):
     row = lax.axis_index("row")
     size = D // n_row
@@ -1233,17 +1366,24 @@
     a = lax.broadcasted_iota(jnp.int32, (HEADS, HEADS), 0)
     b = lax.broadcasted_iota(jnp.int32, (HEADS, HEADS), 1)
     same = jnp.where(a == b, 1.0, 0.0).astype(bf16)
+    low = shard_half(size, 0)[1]
     for layer in range(2):
-        for j in range(3):
+        for j in range(2):
+            qkv_o[layer, :, 2 * D * j : 2 * D * j + D] = qkv_ref[j, layer, 0:size, :].astype(f32)
+        qkv_o[layer, 0:low, D : 2 * D] = qkv_ref[0, layer, size : size + low, :].astype(f32)
+        qkv_o[layer, low:size, D : 2 * D] = qkv_ref[1, layer, size : 2 * size - low, :].astype(f32)
+        proj_o[layer, 0:low, :] = fc1_ref[0, layer, 2 * size : 2 * size + low, :].astype(f32)
+        proj_o[layer, low:size, :] = fc1_ref[1, layer, 2 * size : 3 * size - low, :].astype(f32)
+        for j in range(4):
             at = size * (j % 2)
-            qkv_o[layer, :, D * j : D * (j + 1)] = a_ref[j // 2, layer, at : at + size, :].astype(f32)
-        proj_o[layer] = a_ref[1, layer, size : 2 * size, :].astype(f32)
-        for j in range(4):
-            fc1_o[layer, :, D * j : D * (j + 1)] = m_ref[
-                0, layer, size * j : size * (j + 1), :
+            fc1_o[layer, :, D * j : D * (j + 1)] = fc1_ref[
+                j // 2, layer, at : at + size, :
             ].astype(f32)
-        fc2_o[layer] = m_ref[1, layer, 0 : 4 * size, :].astype(f32)
-        vectors = a_ref[0, layer, 2 * size : 2 * size + 16, :]
+        for j in range(2):
+            fc2_o[layer, 2 * size * j : 2 * size * (j + 1), :] = fc2_ref[
+                j, layer, 0 : 2 * size, :
+            ].astype(f32)
+        vectors = qkv_ref[0, layer, size + low : size + low + 16, :]
         mine = dot_nn(vectors, pick)
         qvb_o[layer] = mine[0:2]
         projb_o[layer : layer + 1] = mine[2:3]
@@ -1252,11 +1392,11 @@
         shift_o[layer] = mine[6:8]
         mine = dot_nn(vectors, pick_fc1)
         fc1b_o[layer : layer + 1] = column_sum(jnp.where(spot == 8 + start // D, mine, 0.0))
-        table = a_ref[1, layer, 2 * size : 2 * size + 16, 0:TABLE_PAD]
+        table = qkv_ref[1, layer, size + low : size + low + 16, 0:TABLE_PAD]
         table_o[layer] = dot_tn(table, same)[0:TABLE, :]
 
 
-def unpack_gradients(final_m, final_a):
+def unpack_gradients(*finals):
     n_row = lax.axis_size("row")
     size = D // n_row
     shapes = [
@@ -1277,7 +1417,7 @@
         out_shape=[jax.ShapeDtypeStruct(shape, f32) for shape in shapes],
         compiler_params=pltpu.CompilerParams(vmem_limit_bytes=VMEM_LIMIT),
         name="unpack_gradients",
-    )(final_m, final_a)
+    )(*finals)
 
 
 def exchange(values):
@@ -1306,42 +1446,23 @@
     tokens = inputs.shape[0]
     block_rows = tokens // (clip_count * row_count)
     grid_rows = tokens // GRID_COLS
-    slot_rows = grid_rows * row_count
     window_rows = grid_rows // WIN
-    part = D // row_count
 
     placing = source_of // tokens * block_rows + source_of % block_rows
     placing = placing.reshape(window_rows, 2, SHIFT, WIN_COLS, 2, SHIFT)
     placing = placing.transpose(0, 3, 1, 4, 2, 5).reshape(tokens)
-    middle = lax.axis_index("row") * grid_rows + WIN * (1 + jnp.arange(window_rows))
-    row_cut = ((middle == split_row[0]) | (middle == slot_rows)).astype(jnp.int32)
-    col_cut = (jnp.arange(WIN_COLS) == WIN_COLS - 1).astype(jnp.int32)
-    cuts = (32 * row_cut[:, None] + 16 * col_cut[None, :]).reshape(-1)
-
-    cuts = jnp.concatenate([jnp.zeros_like(cuts), cuts])
-
-    vectors = jnp.concatenate(
-        [qv_bias, proj_bias[:, None], fc2_bias[:, None], norm_gain, norm_bias], axis=1
-    )
-    vectors = jnp.concatenate(
-        [
-            jnp.pad(vectors, ((0, 0), (0, 0), (0, D - part))),
-            jnp.pad(fc1_bias[:, None], ((0, 0), (0, 7), (0, D - 4 * part))),
-        ],
-        axis=1,
-    ).reshape(32, D)
     if not can_swap(tokens, clip_count * row_count):
         inputs, cotangent = exchange(inputs), exchange(cotangent)
-    saved, upstream, out_rows, full, vec_rows = forward_layers(
-        cuts,
+    saved, upstream, layer_two, full, vec_rows = forward_layers(
+        split_row,
         placing,
         inputs,
         cotangent,
         (qkv_weight, proj_weight, fc1_weight, fc2_weight),
-        vectors,
+        (qv_bias, proj_bias, fc1_bias, fc2_bias, norm_gain, norm_bias),
         rel_table,
     )
-    output, input_grad, *finals = backward_layers(placing, upstream, out_rows, saved, full, vec_rows)
+    output, input_grad, *finals = backward_layers(placing, upstream, layer_two, saved, full, vec_rows)
     if not can_swap(tokens, clip_count * row_count):
         output, input_grad = exchange(output), exchange(input_grad)
     input_grad = input_grad.astype(f32)

time: 251 us -> 216 us (0.86)
  Pallas kernels: 234 us -> 205 us
  local copies, waits for them, and re-layouts: 10.6 us -> 6.16 us
    pallas_call x1, Pallas kernels: 104 us -> 88.8 us  [forward_layers(): pl.pallas_call(functools.partial(forward_kernel, n_row, n_far, swap), gri...]
    pallas_call x1, Pallas kernels: 126 us -> 113 us  [backward_layers(): pl.pallas_call(functools.partial(backward_kernel, n_row, n_far, swap), gr...]
    unnamed x8 -> x5, local copies, waits for them, and re-layouts: 5.24 us -> 4.12 us
where the time goes in v1:
time: 216 us
  Pallas kernels  205 us (95%)
  local copies, waits for them, and re-layouts  6.16 us (3%)
  other arithmetic  3.15 us (1%)
    pallas_call x1, Pallas kernels, backward_layers(): pl.pallas_call(functools.partial(backward_kernel, n_row, n_far, swap), gr...  113 us
    pallas_call x1, Pallas kernels, forward_layers(): pl.pallas_call(functools.partial(forward_kernel, n_row, n_far, swap), gri...  88.8 us

profile of v1, /device:TPU:0, one launch (start us, length us, event | category | flops | bytes accessed | tf_op | source)
XLA Modules:
  0.0 215.7 jit_solution(9588009611719729860)
XLA Ops:
  1.3 0.7 fusion.2
  2.0 0.2 reshape.29
  2.2 0.1 copy.38
  2.3 0.8 reshape_reshape.7.place_row
  3.1 1.6 copy.41.table_ref
  4.6 1.0 reshape_reshape.9.place_col
  5.6 88.8 %forward_layers.1 = (f32[2,1024,384]{2,1,0:T(8,128)}, bf16[2,1024,1152]{2,1,0:T(8,128)(2,1)}, bf16[2,1024,1024]{2,1,0:T(8,128)(2,1)}, bf16[2,1024,384]{2,1,0:T(8...) custom-call(s32[1]{0:T(128)S(6)} %copy.44.split_ref, ...), custom_call_target="tpu_custom_call" | custom-call | tf_op jit(solution)/shard_map/forward_layers/pallas_call | solution.py:799
  94.5 112.6 %backward_layers.1 = (bf16[1024,384]{1,0:T(8,128)(2,1)}, bf16[1024,384]{1,0:T(8,128)(2,1)}, bf16[2,2,192,384]{3,2,1,0:T(8,128)(2,1)}, bf16[2,2,256,384]{3,2,1,0:T(8,128)(2,1)}, bf16[2,2,192,384]{3,2,1,0:T(8,128)(2,1)}) custom-call(s32[1,1024]{1,0:T(1,128)} %reshape_reshape.7.place_row, bf16[1024,384]{1,0:T(8,128)(2,1)} %get-tuple-element.43.up_ref, ...), custom_call_target="tpu_custom_call" | custom-call | tf_op jit(solution)/shard_map/backward_layers/pallas_call | solution.py:1297
  207.0 0.0 copy-start
  207.0 2.5 %convert_element_type.3 = f32[1024,384]{1,0:T(8,128)} convert(bf16[1024,384]{1,0:T(8,128)(2,1)} %get-tuple-element.58) | non-fusion elementwise | flops 393216 | bytes 2359296 | tf_op jit(solution)/shard_map/convert_element_type | solution.py:1468
  209.5 3.7 %unpack_gradients.1 = (f32[2,96,1152]{2,1,0:T(8,128)}, f32[2,2,96]{2,1,0:T(2,128)}, f32[2,96,384]{2,1,0:T(8,128)}, f32[2,96]{1,0:T(2,128)}, f32[2,96,1536]{2,1,0...) custom-call(bf16[2,2,192,384]{3,2,1,0:T(8,128)(2,1)} %get-tuple-elem, ...), custom_call_target="tpu_custom_call" | custom-call | tf_op jit(solution)/shard_map/unpack_gradients/pallas_call | solution.py:1415
  213.2 1.7 copy.42
  214.8 0.0 copy-done
  214.8 0.9 copy.45
Async XLA Ops:
  207.0 7.8 %copy-start = (bf16[1024,384]{1,0:T(8,128)(2,1)S(1)}, bf16[1024,384]{1,0:T(8,128)(2,1)}, u32[]{:S(2)}) copy-start(bf16[1024,384]{1,0:T(8,128)(2,1)} %get-tuple-element.112) | copy-start | bytes 2359300

commit v2 on v1

--- a/solution.py
+++ b/solution.py
@@ -586,12 +586,8 @@
             vector_copy(d).start()
         mine = pltpu.make_async_copy(vec_mine, vec_got.at[place.row], out_sem.at[4])
         mine.start()
-        eye = lax.broadcasted_iota(jnp.int32, (TABLE, TABLE_PAD), 0) == lax.broadcasted_iota(
-            jnp.int32, (TABLE, TABLE_PAD), 1
-        )
-        eye = jnp.where(eye, 1.0, 0.0).astype(bf16)
-        for l in range(2):
-            table_s[l] = sum(dot_tn(part, eye) for part in reversed(split(table_ref[l])))
+        table_s[...] = jnp.zeros_like(table_s)
+        table_s[:, :, 0:TABLE] = table_ref[...]
         bias_rows(table_s, lanes_ref, order_ref, bias_s, wide_s)
         mine.wait()
         for d in range(1, n_row):
@@ -619,18 +615,16 @@
     @pl.when(step == 1)
     def _():
         pass_weights(0, 1)
+        start_weights(1, 1)
 
     @pl.when(step == chunks - 1)
     def _():
         pass_relayed(0, 1)
-        start_weights(1, 1)
 
     @pl.when(step == chunks)
     def _():
         wait_weights(0, 1)
         pass_weights(1, 0)
-        if swap:
-            swap_start(place, c_in, c_got, c_sem)
 
     @pl.when(step == chunks + 2)
     def _():
@@ -656,6 +650,14 @@
         wait_weights(1, 1)
         for w in range(4):
             pltpu.make_async_copy(kept[w], outs[w], out_sem.at[w]).start()
+
+    @pl.when(step == 2 * chunks - 1)
+    def _():
+        if swap:
+            swap_start(place, c_in, c_got, c_sem)
+
+    @pl.when(step == 4 * chunks - 2)
+    def _():
         if swap:
             swap_wait(place, c_in, c_got, c_sem)
             swap_own(place, c_in, c_got, c_sem).wait()
@@ -674,28 +676,33 @@
         qkv_out[0] = (dot_nn(hidden, qkv_s[layer]) + qkv_b[layer]).astype(bf16)
         wide = (CELL, GROUP * CELL)
         apart = lax.broadcasted_iota(jnp.int32, wide, 0) ^ lax.broadcasted_iota(jnp.int32, wide, 1)
-        for k in range(CHUNK_WINS):
-            rows = slice(CELL * k, CELL * (k + 1))
-            window = chunk * CHUNK_WINS + k
-            middle = (place.row * window_rows + window // WIN_COLS + 1) * WIN
-            row_cut = (middle == split_ref[0]) | (middle == n_row * window_rows * WIN)
-            col_cut = window % WIN_COLS == WIN_COLS - 1
-            cut = layer * (jnp.where(row_cut, 32, 0) + jnp.where(col_cut, 16, 0))
-            keep = (apart & cut) == 0
-            mixed = []
-            for g in range(2):
-                q = qkv_out[0, rows, 128 * g : 128 * g + 256]
+        for first in range(0, CHUNK_WINS, 4):
+            spots = [(k, g) for k in range(first, first + 4) for g in range(2)]
+            scores, probs, mixed = {}, {}, {}
+            for k, g in spots:
+                rows = slice(CELL * k, CELL * (k + 1))
                 key = qkv_out[0, rows, D + 128 * g : D + 128 * g + 256]
-                val = qkv_out[0, rows, 2 * D + 128 * g : 2 * D + 128 * g + 256]
-                q_wide = jnp.concatenate([q] * GROUP, axis=0) * wide_heads_ref[g]
+                scores[k, g] = dot_nt(key, widen_heads(qkv_out[0, rows, 128 * g : 128 * g + 256], wide_heads_ref, g))
+            for k, g in spots:
+                window = chunk * CHUNK_WINS + k
+                middle = (place.row * window_rows + window // WIN_COLS + 1) * WIN
+                row_cut = (middle == split_ref[0]) | (middle == n_row * window_rows * WIN)
+                col_cut = window % WIN_COLS == WIN_COLS - 1
+                cut = layer * (jnp.where(row_cut, 32, 0) + jnp.where(col_cut, 16, 0))
                 lanes = slice(GROUP * CELL * g, GROUP * CELL * (g + 1))
-                scores = dot_nt(key, q_wide) * SCALE + bias_s[layer, :, lanes]
-                scores = jnp.where(keep, scores, MASKED)
-                e = jnp.exp(scores - jnp.max(scores, axis=0, keepdims=True))
+                score = scores[k, g] * SCALE + bias_s[layer, :, lanes]
+                score = jnp.where((apart & cut) == 0, score, MASKED)
+                e = jnp.exp(score - jnp.max(score, axis=0, keepdims=True))
                 prob = (e * (1.0 / jnp.sum(e, axis=0, keepdims=True))).astype(bf16)
-                prob_out[0, rows, lanes] = prob
-                mixed.append(gather_heads(dot_tn(prob, val), heads_ref, g))
-            att_out[0, rows, :] = join_groups(*mixed).astype(bf16)
+                prob_out[0, CELL * k : CELL * (k + 1), lanes] = prob
+                probs[k, g] = prob
+            for k, g in spots:
+                val = qkv_out[0, CELL * k : CELL * (k + 1), 2 * D + 128 * g : 2 * D + 128 * g + 256]
+                mixed[k, g] = gather_heads(dot_tn(probs[k, g], val), heads_ref, g)
+            for k in range(first, first + 4):
+                att_out[0, CELL * k : CELL * (k + 1), :] = join_groups(
+                    mixed[k, 0], mixed[k, 1]
+                ).astype(bf16)
         mid = x + (dot_nn(att_out[0], proj_s[layer]) + vec_out[layer, 2:3, :])
         x_s[here, :] = mid
         mid_out[0] = mid
@@ -743,13 +750,40 @@
 
 
 def gather_heads(spread, heads_ref, g):
-    total = None
+    tiles = []
+    for tile in range(2):
+        lanes = slice(128 * tile, 128 * (tile + 1))
+        first = 128 * (g + tile)
+        total = None
+        for h in range(GROUP):
+            head = GROUP * g + h
+            if HEAD_DIM * head >= first + 128 or HEAD_DIM * (head + 1) <= first:
+                continue
+            part = (
+                spread[CELL * h : CELL * (h + 1), lanes]
+                * heads_ref[head : head + 1, first : first + 128]
+            )
+            total = part if total is None else total + part
+        tiles.append(total)
+    return jnp.concatenate(tiles, axis=1)
+
+
+def widen_heads(values, wide_heads_ref, g):
+    rows = []
     for h in range(GROUP):
-        part = spread[CELL * h : CELL * (h + 1), :] * heads_ref[
-            GROUP * g + h : GROUP * g + h + 1, 128 * g : 128 * g + 256
-        ]
-        total = part if total is None else total + part
-    return total
+        head = GROUP * g + h
+        tiles = []
+        for tile in range(2):
+            first = 128 * (g + tile)
+            if HEAD_DIM * head >= first + 128 or HEAD_DIM * (head + 1) <= first:
+                tiles.append(jnp.zeros((CELL, 128), bf16))
+            else:
+                lanes = slice(128 * tile, 128 * (tile + 1))
+                tiles.append(
+                    values[:, lanes] * wide_heads_ref[g, CELL * h : CELL * (h + 1), lanes]
+                )
+        rows.append(jnp.concatenate(tiles, axis=1))
+    return jnp.concatenate(rows, axis=0)
 
 
 def join_groups(low, high):
@@ -769,7 +803,7 @@
     patches = anywhere if swap else whole((tokens, D))
     small = (
         *vectors,
-        rel_table,
+        rel_table.transpose(0, 2, 1),
         jnp.asarray(lanes.reshape(2 * TABLE_PAD, 128), dtype=bf16),
         jnp.asarray(order, dtype=bf16),
         jnp.asarray(heads),
@@ -1143,30 +1177,41 @@
     @pl.when(kind == 1)
     def _():
         att_grad = dot_nt(ga_s[here, :], proj_w[0]).astype(bf16)
-        for k in range(CHUNK_WINS):
-            rows = slice(CELL * k, CELL * (k + 1))
-            there = pl.ds(pl.multiple_of(chunk * CHUNK + CELL * k, CELL), CELL)
-            q_parts, k_parts, v_parts = [], [], []
-            for g in range(2):
-                q = qkv_ref[0, rows, 128 * g : 128 * g + 256]
-                key = qkv_ref[0, rows, D + 128 * g : D + 128 * g + 256]
-                val = qkv_ref[0, rows, 2 * D + 128 * g : 2 * D + 128 * g + 256]
-                do = att_grad[rows, 128 * g : 128 * g + 256]
-                q_wide = jnp.concatenate([q] * GROUP, axis=0) * wide_heads_ref[g]
-                do_wide = jnp.concatenate([do] * GROUP, axis=0) * wide_heads_ref[g]
-                lanes = slice(GROUP * CELL * g, GROUP * CELL * (g + 1))
-                prob_low = prob_ref[0, rows, lanes]
+        table = [jnp.zeros((CELL, GROUP * CELL), f32) for _ in range(2)]
+        for first in range(0, CHUNK_WINS, 4):
+            spots = [(k, g) for k in range(first, first + 4) for g in range(2)]
+            do_wides, dps, dss, parts = {}, {}, {}, {}
+
+            def piece(k, g, at):
+                return qkv_ref[
+                    0, CELL * k : CELL * (k + 1), D * at + 128 * g : D * at + 128 * g + 256
+                ]
+
+            for k, g in spots:
+                do = att_grad[CELL * k : CELL * (k + 1), 128 * g : 128 * g + 256]
+                do_wides[k, g] = widen_heads(do, wide_heads_ref, g)
+                val = piece(k, g, 2)
+                dps[k, g] = dot_nt(val, do_wides[k, g])
+            for k, g in spots:
+                prob_low = prob_ref[
+                    0, CELL * k : CELL * (k + 1), GROUP * CELL * g : GROUP * CELL * (g + 1)
+                ]
                 prob = prob_low.astype(f32)
-                dp = dot_nt(val, do_wide)
-                v_parts.append(dot_nn(prob_low, do_wide))
-                weighted = prob * dp
+                weighted = prob * dps[k, g]
                 ds = (weighted - prob * column_sum(weighted)).astype(bf16)
-                table_g[:, lanes] += ds.astype(f32)
-                k_parts.append(dot_nn(ds, q_wide))
-                q_parts.append(gather_heads(dot_tn(ds, key), heads_ref, g))
-            dt_s[there, 0:D] = (join_groups(*q_parts) * SCALE).astype(bf16)
-            dt_s[there, D : 2 * D] = (join_groups(*k_parts) * SCALE).astype(bf16)
-            dt_s[there, 2 * D : 3 * D] = join_groups(*v_parts).astype(bf16)
+                table[g] += ds.astype(f32)
+                dss[k, g] = ds
+                parts[k, g, 2] = dot_nn(prob_low, do_wides[k, g])
+            for k, g in spots:
+                parts[k, g, 0] = gather_heads(dot_tn(dss[k, g], piece(k, g, 1)), heads_ref, g)
+                parts[k, g, 1] = dot_nn(dss[k, g], widen_heads(piece(k, g, 0), wide_heads_ref, g))
+            for k in range(first, first + 4):
+                there = pl.ds(pl.multiple_of(chunk * CHUNK + CELL * k, CELL), CELL)
+                for at, factor in enumerate((SCALE, SCALE, 1.0)):
+                    joined = join_groups(parts[k, 0, at], parts[k, 1, at]) * factor
+                    dt_s[there, D * at : D * (at + 1)] = joined.astype(bf16)
+        for g in range(2):
+            table_g[:, GROUP * CELL * g : GROUP * CELL * (g + 1)] += table[g]
         dt = dt_s[here, :]
         vec_g[0:1, :] += column_sum(dt[:, 0:D].astype(f32))
         vec_g[1:2, :] += column_sum(dt[:, 2 * D :].astype(f32))
@@ -1191,6 +1236,8 @@
     def _():
         for b in (4, 3, 2):
             advance(b)
+        unpick_rows(g_s[0].astype(bf16), grad_rows)
+        start_rows(grad_rows, grad_out, grad_sem)
 
     @pl.when(step % (2 * chunks) == 2 * chunks - 1)
     def _():
@@ -1218,8 +1265,6 @@
     @pl.when(step == 4 * chunks - 1)
     def _():
         copy_a(5).start()
-        unpick_rows(g_s[0].astype(bf16), grad_rows)
-        start_rows(grad_rows, grad_out, grad_sem)
         while min(reached) < len(stages):
             for b in (5, 4, 3, 2, 1, 0):
                 advance(b)
@@ -1350,55 +1395,73 @@
     )(placing.reshape(1, tokens), upstream, y, x, qkv, prob, att, mid, act, slope, *full, *constants)
 
 
-def unpack_kernel(
-    n_row, fc2_ref, fc1_ref, qkv_ref, qkv_o, qvb_o, proj_o, projb_o, fc1_o, fc1b_o, fc2_o, fc2b_o, gain_o, shift_o, table_o
+def close_kernel(
+    n_row,
+    fc2_ref,
+    fc1_ref,
+    qkv_ref,
+    rows_ref,
+    grad_ref,
+    rows_o,
+    grad_o,
+    qkv_o,
+    qvb_o,
+    proj_o,
+    projb_o,
+    fc1_o,
+    fc1b_o,
+    fc2_o,
+    fc2b_o,
+    gain_o,
+    shift_o,
+    table_o,
 ):
+    rows_o[...] = rows_ref[...]
+    grad_o[...] = grad_ref[...].astype(f32)
     row = lax.axis_index("row")
-    size = D // n_row
+    size = row_share(n_row)
+    low = shard_half(size, 0)[1]
+    layer = pl.program_id(0)
+    for j in range(2):
+        qkv_o[0, :, 2 * D * j : 2 * D * j + D] = qkv_ref[j, 0, 0:size, :].astype(f32)
+    qkv_o[0, 0:low, D : 2 * D] = qkv_ref[0, 0, size : size + low, :].astype(f32)
+    qkv_o[0, low:size, D : 2 * D] = qkv_ref[1, 0, size : 2 * size - low, :].astype(f32)
+    proj_o[0, 0:low, :] = fc1_ref[0, 0, 2 * size : 2 * size + low, :].astype(f32)
+    proj_o[0, low:size, :] = fc1_ref[1, 0, 2 * size : 3 * size - low, :].astype(f32)
+    for j in range(4):
+        at = size * (j % 2)
+        fc1_o[0, :, D * j : D * (j + 1)] = fc1_ref[j // 2, 0, at : at + size, :].astype(f32)
+    for j in range(2):
+        fc2_o[0, 2 * size * j : 2 * size * (j + 1), :] = fc2_ref[j, 0, 0 : 2 * size, :].astype(f32)
+    vectors = qkv_ref[0, 0, size + low : size + low + 16, :]
     lane = lax.broadcasted_iota(jnp.int32, (D, size), 0)
     want = lax.broadcasted_iota(jnp.int32, (D, size), 1)
-    pick = jnp.where(lane == want + size * row, 1.0, 0.0).astype(bf16)
+    mine = dot_nn(vectors, jnp.where(lane == want + size * row, 1.0, 0.0).astype(bf16))
     start = 4 * size * row
     lane = lax.broadcasted_iota(jnp.int32, (D, 4 * size), 0)
     want = lax.broadcasted_iota(jnp.int32, (D, 4 * size), 1)
-    pick_fc1 = jnp.where(lane == want + start % D, 1.0, 0.0).astype(bf16)
     spot = lax.broadcasted_iota(jnp.int32, (16, 4 * size), 0)
-    a = lax.broadcasted_iota(jnp.int32, (HEADS, HEADS), 0)
-    b = lax.broadcasted_iota(jnp.int32, (HEADS, HEADS), 1)
-    same = jnp.where(a == b, 1.0, 0.0).astype(bf16)
-    low = shard_half(size, 0)[1]
-    for layer in range(2):
-        for j in range(2):
-            qkv_o[layer, :, 2 * D * j : 2 * D * j + D] = qkv_ref[j, layer, 0:size, :].astype(f32)
-        qkv_o[layer, 0:low, D : 2 * D] = qkv_ref[0, layer, size : size + low, :].astype(f32)
-        qkv_o[layer, low:size, D : 2 * D] = qkv_ref[1, layer, size : 2 * size - low, :].astype(f32)
-        proj_o[layer, 0:low, :] = fc1_ref[0, layer, 2 * size : 2 * size + low, :].astype(f32)
-        proj_o[layer, low:size, :] = fc1_ref[1, layer, 2 * size : 3 * size - low, :].astype(f32)
-        for j in range(4):
-            at = size * (j % 2)
-            fc1_o[layer, :, D * j : D * (j + 1)] = fc1_ref[
-                j // 2, layer, at : at + size, :
-            ].astype(f32)
-        for j in range(2):
-            fc2_o[layer, 2 * size * j : 2 * size * (j + 1), :] = fc2_ref[
-                j, layer, 0 : 2 * size, :
-            ].astype(f32)
-        vectors = qkv_ref[0, layer, size + low : size + low + 16, :]
-        mine = dot_nn(vectors, pick)
-        qvb_o[layer] = mine[0:2]
-        projb_o[layer : layer + 1] = mine[2:3]
-        fc2b_o[layer : layer + 1] = mine[3:4]
-        gain_o[layer] = mine[4:6]
-        shift_o[layer] = mine[6:8]
-        mine = dot_nn(vectors, pick_fc1)
-        fc1b_o[layer : layer + 1] = column_sum(jnp.where(spot == 8 + start // D, mine, 0.0))
-        table = qkv_ref[1, layer, size + low : size + low + 16, 0:TABLE_PAD]
-        table_o[layer] = dot_tn(table, same)[0:TABLE, :]
-
-
-def unpack_gradients(*finals):
+    wide = dot_nn(vectors, jnp.where(lane == want + start % D, 1.0, 0.0).astype(bf16))
+    wide = column_sum(jnp.where(spot == 8 + start // D, wide, 0.0))
+    qvb_o[0] = mine[0:2]
+    gain_o[0] = mine[4:6]
+    shift_o[0] = mine[6:8]
+    for at in range(2):
+
+        @pl.when(layer == at)
+        def _():
+            projb_o[at : at + 1, :] = mine[2:3]
+            fc2b_o[at : at + 1, :] = mine[3:4]
+            fc1b_o[at : at + 1, :] = wide
+
+    table_o[0] = qkv_ref[1, 0, size + low : size + low + 16, 0:TABLE].astype(f32)
+
+
+def close(rows, grads, finals):
     n_row = lax.axis_size("row")
-    size = D // n_row
+    size = row_share(n_row)
+    tokens = rows.shape[0]
+    half = tokens // 2
     shapes = [
         (2, size, 3 * D),
         (2, 2, size),
@@ -1410,14 +1473,30 @@
         (2, size),
         (2, 2, size),
         (2, 2, size),
-        (2, TABLE, HEADS),
+        (2, HEADS, TABLE),
     ]
+
+    def layered(shape):
+        if len(shape) == 2:
+            return whole(shape)
+        return pl.BlockSpec((1, *shape[1:]), lambda i: (i, 0, 0))
+
     return pl.pallas_call(
-        functools.partial(unpack_kernel, n_row),
-        out_shape=[jax.ShapeDtypeStruct(shape, f32) for shape in shapes],
+        functools.partial(close_kernel, n_row),
+        grid=(2,),
+        in_specs=[
+            pl.BlockSpec((2, 1, *final.shape[2:]), lambda i: (0, i, 0, 0)) for final in finals
+        ]
+        + [rows_of((half, D))] * 2,
+        out_specs=[rows_of((half, D))] * 2 + [layered(shape) for shape in shapes],
+        out_shape=[
+            jax.ShapeDtypeStruct((tokens, D), bf16),
+            jax.ShapeDtypeStruct((tokens, D), f32),
+        ]
+        + [jax.ShapeDtypeStruct(shape, f32) for shape in shapes],
         compiler_params=pltpu.CompilerParams(vmem_limit_bytes=VMEM_LIMIT),
-        name="unpack_gradients",
-    )(*finals)
+        name="close",
+    )(*finals, rows, grads)
 
 
 def exchange(values):
@@ -1465,8 +1544,8 @@
     output, input_grad, *finals = backward_layers(placing, upstream, layer_two, saved, full, vec_rows)
     if not can_swap(tokens, clip_count * row_count):
         output, input_grad = exchange(output), exchange(input_grad)
-    input_grad = input_grad.astype(f32)
-    totals = unpack_gradients(*finals)
+    output, input_grad, *totals = close(output, input_grad, finals)
+    totals[-1] = totals[-1].transpose(0, 2, 1)
     return (output, input_grad, *totals)
 
 

time: 216 us -> 200 us (0.926)
  Pallas kernels: 205 us -> 195 us
  local copies, waits for them, and re-layouts: 6.16 us -> 2.04 us
  other arithmetic: 3.15 us -> 0.7 us
    pallas_call x1, Pallas kernels: 88.8 us -> 83 us  [forward_layers(): pl.pallas_call(functools.partial(forward_kernel, n_row, n_far, swap), gri...]
    pallas_call x1, Pallas kernels: 113 us -> 108 us  [backward_layers(): pl.pallas_call(functools.partial(backward_kernel, n_row, n_far, swap), gr...]
    unnamed x5 -> x0, local copies, waits for them, and re-layouts: 4.12 us -> none
    convert_element_type x1 -> x0, other arithmetic: 2.45 us -> none  [body(): input_grad = input_grad.astype(f32)]
where the time goes in v2:
time: 200 us; the launch traced here: 199 us
  Pallas kernels  195 us (98%)
  local copies, waits for them, and re-layouts  2.04 us (1%)
    pallas_call x1, Pallas kernels, backward_layers(): pl.pallas_call(functools.partial(backward_kernel, n_row, n_far, swap), gr...  108 us
    pallas_call x1, Pallas kernels, forward_layers(): pl.pallas_call(functools.partial(forward_kernel, n_row, n_far, swap), gri...  83 us
    pallas_call x1, Pallas kernels, close(): pl.pallas_call(functools.partial(close_kernel, n_row), grid=(2,), in_spec...  4.42 us

profile of v2, /device:TPU:0, one launch (start us, length us, event | category | flops | bytes accessed | tf_op | source)
XLA Modules:
  0.0 199.3 jit_solution(13516016769253955458)
XLA Ops:
  1.3 0.7 fusion.2
  2.0 0.2 reshape.29
  2.2 0.1 copy.36
  2.3 0.8 reshape_reshape.7.place_row
  3.1 1.0 reshape_reshape.9.place_col
  4.0 83.0 %forward_layers.1 = (f32[2,1024,384]{2,1,0:T(8,128)}, bf16[2,1024,1152]{2,1,0:T(8,128)(2,1)}, bf16[2,1024,1024]{2,1,0:T(8,128)(2,1)}, bf16[2,1024,384]{2,1,0:T(8...) custom-call(s32[1]{0:T(128)S(6)} %copy.39.split_ref, ...), custom_call_target="tpu_custom_call" | custom-call | tf_op jit(solution)/shard_map/forward_layers/pallas_call | solution.py:833
  87.1 107.7 %backward_layers.1 = (bf16[1024,384]{1,0:T(8,128)(2,1)}, bf16[1024,384]{1,0:T(8,128)(2,1)}, bf16[2,2,192,384]{3,2,1,0:T(8,128)(2,1)}, bf16[2,2,256,384]{3,2,1,0:T(8,128)(2,1)}, bf16[2,2,192,384]{3,2,1,0:T(8,128)(2,1)}) custom-call(s32[1,1024]{1,0:T(1,128)} %reshape_reshape.7.place_row, bf16[1024,384]{1,0:T(8,128)(2,1)} %get-tuple-element.45.up_ref, ...), custom_call_target="tpu_custom_call" | custom-call | tf_op jit(solution)/shard_map/backward_layers/pallas_call | solution.py:1342
  194.7 4.4 %close.1 = (bf16[1024,384]{1,0:T(8,128)(2,1)}, f32[1024,384]{1,0:T(8,128)}, f32[2,96,1152]{2,1,0:T(8,128)}, f32[2,2,96]{2,1,0:T(2,128)}, f32[2,96,384]{2,1,0:T(8...) custom-call(bf16[2,2,192,384]{3,2,1,0:T(8,128)(2,1)} %get-tuple-elem, ...), custom_call_target="tpu_custom_call" | custom-call | tf_op jit(solution)/shard_map/close/pallas_call | solution.py:1484

commit v3 on v2

--- a/solution.py
+++ b/solution.py
@@ -271,7 +271,7 @@
     return tokens // n % 16 == 0
 
 
-def meet_all(place):
+def meet_all(place, meanwhile):
     barrier = pltpu.get_barrier_semaphore()
 
     def greet(d, carry):
@@ -279,6 +279,7 @@
         return carry
 
     lax.fori_loop(1, place.n, greet, 0)
+    meanwhile()
     pl.semaphore_wait(barrier, place.n - 1)
 
 
@@ -557,15 +558,19 @@
 
     @pl.when(step == 0)
     def _():
-        for l in range(2):
-            for w in range(4):
-                own(l, w).start()
+        def start_own():
+            for l in range(2):
+                for w in range(4):
+                    own(l, w).start()
+            if swap:
+                swap_own(place, x_in, x_got, x_sem).start()
+                swap_own(place, c_in, c_got, c_sem).start()
+
         if swap:
-            swap_own(place, x_in, x_got, x_sem).start()
-            swap_own(place, c_in, c_got, c_sem).start()
-            meet_all(place)
+            meet_all(place, start_own)
             swap_start(place, x_in, x_got, x_sem)
         else:
+            start_own()
             meet(place.partners(far=False))
         start_weights(0, 0)
         vec_wide[...] = jnp.zeros_like(vec_wide)
@@ -1077,6 +1082,7 @@
         3 * chunks: (2,),
         3 * chunks + 1: (1, 4),
         3 * chunks + 2: (2, 3),
+        3 * chunks + 3: (4,),
     }
     reached = [0] * len(BATCHES)
 
@@ -1087,12 +1093,15 @@
 
     @pl.when(step == 0)
     def _():
+        def widen_up():
+            g_s[1] = up_ref[...].astype(f32)
+
         if swap:
-            meet_all(place)
+            meet_all(place, widen_up)
         else:
+            widen_up()
             meet(place.partners())
         start_rows(rows_in, rows_out, rows_sem)
-        g_s[1] = up_ref[...].astype(f32)
         for k in range(3):
             valid, padded = batch_rows(n_row, k), out_cs[k].shape[1]
             if padded > valid:
@@ -1234,7 +1243,7 @@
 
     @pl.when(step == 4 * chunks - 1)
     def _():
-        for b in (4, 3, 2):
+        for b in (3, 2):
             advance(b)
         unpick_rows(g_s[0].astype(bf16), grad_rows)
         start_rows(grad_rows, grad_out, grad_sem)

time: 200 us -> 200 us (level)
  no operation moved by 1% of the time
where the time goes in v3:
time: 200 us
  Pallas kernels  196 us (98%)
  local copies, waits for them, and re-layouts  2.04 us (1%)
    pallas_call x1, Pallas kernels, backward_layers(): pl.pallas_call(functools.partial(backward_kernel, n_row, n_far, swap), gr...  107 us
    pallas_call x1, Pallas kernels, forward_layers(): pl.pallas_call(functools.partial(forward_kernel, n_row, n_far, swap), gri...  84.9 us
    pallas_call x1, Pallas kernels, close(): pl.pallas_call(functools.partial(close_kernel, n_row), grid=(2,), in_spec...  4.42 us

profile of v3, /device:TPU:0, one launch (start us, length us, event | category | flops | bytes accessed | tf_op | source)
XLA Modules:
  0.0 200.0 jit_solution(9197397230550879092)
XLA Ops:
  1.3 0.7 fusion.2
  2.0 0.2 reshape.29
  2.2 0.1 copy.36
  2.3 0.8 reshape_reshape.7.place_row
  3.1 1.0 reshape_reshape.9.place_col
  4.0 84.9 %forward_layers.1 = (f32[2,1024,384]{2,1,0:T(8,128)}, bf16[2,1024,1152]{2,1,0:T(8,128)(2,1)}, bf16[2,1024,1024]{2,1,0:T(8,128)(2,1)}, bf16[2,1024,384]{2,1,0:T(8...) custom-call(s32[1]{0:T(128)S(6)} %copy.39.split_ref, ...), custom_call_target="tpu_custom_call" | custom-call | tf_op jit(solution)/shard_map/forward_layers/pallas_call | solution.py:838
  88.9 106.5 %backward_layers.1 = (bf16[1024,384]{1,0:T(8,128)(2,1)}, bf16[1024,384]{1,0:T(8,128)(2,1)}, bf16[2,2,192,384]{3,2,1,0:T(8,128)(2,1)}, bf16[2,2,256,384]{3,2,1,0:T(8,128)(2,1)}, bf16[2,2,192,384]{3,2,1,0:T(8,128)(2,1)}) custom-call(s32[1,1024]{1,0:T(1,128)} %reshape_reshape.7.place_row, bf16[1024,384]{1,0:T(8,128)(2,1)} %get-tuple-element.45.up_ref, ...), custom_call_target="tpu_custom_call" | custom-call | tf_op jit(solution)/shard_map/backward_layers/pallas_call | solution.py:1351
  195.4 4.4 %close.1 = (bf16[1024,384]{1,0:T(8,128)(2,1)}, f32[1024,384]{1,0:T(8,128)}, f32[2,96,1152]{2,1,0:T(8,128)}, f32[2,2,96]{2,1,0:T(2,128)}, f32[2,96,384]{2,1,0:T(8...) custom-call(bf16[2,2,192,384]{3,2,1,0:T(8,128)(2,1)} %get-tuple-elem, ...), custom_call_target="tpu_custom_call" | custom-call | tf_op jit(solution)/shard_map/close/pallas_call | solution.py:1493
